TPU v7x, 256 devices: a whole 4x4x8 slice. The times are simulated.
256 devices in a mesh: ctx: 64 (over x, z, y_lo), ts: 4 (over y_hi, core).
Axes of the slice: x: 4, y: 4 (y_hi: 2, y_lo: 2; y = y_hi * 2 + y_lo), z: 8, core: 2. Of those that a mesh axis runs over, the one named last changes fastest.
Arguments:
- se_input: bfloat16 [16384, 3, 4096], P('ctx', None, 'ts'), may hold values from -6 to 6
- mr_input: bfloat16 [16384, 2, 4096], P('ctx', None, 'ts'), may hold values from -6 to 6
- cotangent: bfloat16 [16384, 4096], P('ctx', 'ts'), may hold values from -6 to 6
- se_featurizer: float32 [3, 3, 4096], P(None, None, 'ts'), may hold values from -3.5 to 3.5
- mr_featurizer: float32 [3, 3, 4096], P(None, None, 'ts'), may hold values from -3.5 to 3.5
- se_filter: float32 [7, 4096], P(None, 'ts'), may hold values from -2 to 2
- mr_filter: float32 [128, 4096], P(None, 'ts'), may hold values from -1 to 1
- decay_rate: float32 [4096], P('ts'), may hold values from 0.003 to 0.05
Outputs:
- grad_se_input: bfloat16 [16384, 3, 4096], P('ctx', None, 'ts')
- grad_mr_input: bfloat16 [16384, 2, 4096], P('ctx', None, 'ts')
- grad_se_filter: float32 [7, 4096], P(None, 'ts')
- grad_mr_filter: float32 [128, 4096], P(None, 'ts')
All inputs are finite; a program needn't handle non-finite values.
Results may differ from a plain program's by a relative error of at most 0.0061.
Values may be sent and summed in bfloat16 or wider, within the bound.
No kernel may reach another device: no remote copies, remote signals or barrier semaphores. Data moves between devices by JAX's collectives and lax.ppermute only.
A program may use at most 128 MiB of HBM per device.

v0:
```python
import functools
import math

import jax
import jax.numpy as jnp
import ml_dtypes
import numpy as np
from jax import lax
from jax.experimental import pallas as pl
from jax.experimental.pallas import tpu as pltpu
from jax.sharding import PartitionSpec as P

F32 = jnp.float32
BF16 = jnp.bfloat16
LANES = 128
BLOCK = 256
PAD = 16
REACH = 16
POINTS = 400
HALF = POINTS // 2
DEPTH = 512


def chunks(begin, end, step=32):
    return [(a, min(step, end - a)) for a in range(begin, end, step)]


def split(value):
    high = value.astype(BF16)
    return high, (value - high.astype(F32)).astype(BF16)


def transform_tables():
    frequency = (np.arange(HALF) + 0.5)[:, None]

    def table_at(places):
        angle = 2.0 * np.pi * frequency * places[None, :] / POINTS
        return np.concatenate([np.cos(angle), -np.sin(angle)], axis=0)

    forward = table_at(np.arange(POINTS))
    behind = table_at(np.concatenate([np.arange(-128, 0), np.arange(256, 256 + REACH)]))
    back = forward.T[: 256 + REACH]
    tables = []
    for table, depth in ((forward, DEPTH), (behind, 256), (back, DEPTH)):
        table = np.pad(table, ((0, 0), (0, depth - table.shape[1])))
        high = table.astype(ml_dtypes.bfloat16)
        low = (table - high.astype(np.float64)).astype(ml_dtypes.bfloat16)
        tables.append(np.stack([high, low]))
    return tables


def weighted(ref, lead, row, count, taps, step):
    total = ref[lead + (pl.ds(row, count), slice(None))] * taps[0]
    for j in range(1, len(taps)):
        total = total + ref[lead + (pl.ds(row + step * j, count), slice(None))] * taps[j]
    return total


def rounded(value):
    return value.astype(BF16).astype(F32)


def dot(a, b):
    return jnp.dot(a, b, preferred_element_type=F32)


def wide_dot(table, rows, columns, value):
    high, low = split(value)
    return (
        dot(table[0, rows, columns], high)
        + dot(table[1, rows, columns], high)
        + dot(table[0, rows, columns], low)
    )


def lanes_of(h):
    return slice(h * LANES, (h + 1) * LANES)


def feature_taps(ref, lanes):
    return [[ref[j, p, lanes][None, :] for j in range(3)] for p in range(3)]


def short_taps(ref, lanes):
    return [ref[j, lanes][None, :] for j in range(7)]


def product_of(first, second, conjugate):
    fr, fi = first[:HALF, :], first[HALF:, :]
    sr, si = second[:HALF, :], second[HALF:, :]
    zeros = jnp.zeros((DEPTH - POINTS, BLOCK), F32)
    if conjugate:
        return jnp.concatenate([fr * sr + fi * si, fr * si - fi * sr, zeros], axis=0)
    return jnp.concatenate([fr * sr - fi * si, fr * si + fi * sr, zeros], axis=0)


def edge_kernel(
    se_start, se_end, mr_start, mr_end, g_ref, sw_ref, mw_ref, sf_ref, last_ref, first_ref, x, q1, ps, y1, tail
):
    for h in range(g_ref.shape[1] // LANES):
        lanes = lanes_of(h)
        sw = feature_taps(sw_ref, lanes)
        mw = feature_taps(mw_ref, lanes)
        sf = short_taps(sf_ref, lanes)
        x[3, 0:PAD, :] = jnp.zeros((PAD, LANES), F32)
        for a, n in chunks(0, 144):
            x[3, pl.ds(PAD + a, n), :] = mr_start[0, pl.ds(a, n), lanes].astype(F32)
        for a, n in chunks(0, 144):
            q2 = weighted(x, (3,), PAD + a, n, mw[0], -1)
            first_ref[pl.ds(a, n), lanes] = (
                g_ref[pl.ds(a, n), lanes].astype(F32) * q2
            ).astype(BF16)
        for p in range(3):
            x[p, 0:16, :] = se_start[p, :, lanes].astype(F32)
        x[4, 0:16, :] = mr_start[1, 0:16, lanes].astype(F32)
        y1[0:16, :] = g_ref[0:16, lanes].astype(F32)
        tail[...] = jnp.zeros((32, LANES), F32)
        tail[0:2, :] = y1[0:2, :]
        tail[2:4, :] = x[3, PAD : PAD + 2, :]
        tail[4:14, :] = x[4, 0:10, :]
        tail[14:22, :] = x[0, 0:8, :]
        tail[22:24, :] = x[1, 0:2, :]
        tail[24:26, :] = x[2, 0:2, :]
        first_ref[144:176, lanes] = tail[...].astype(BF16)

        for p in range(3):
            x[p, 0:32, :] = se_end[p, :, lanes].astype(F32)
        for p in range(2):
            x[3 + p, 0:32, :] = mr_end[p, :, lanes].astype(F32)
        k1 = weighted(x, (1,), 8, 24, sw[1], -1)
        v1 = weighted(x, (2,), 8, 24, sw[2], -1)
        ps[8:32, :] = rounded(k1 * v1)
        q1[8:32, :] = weighted(x, (0,), 8, 24, sw[0], -1)
        y1[16:32, :] = rounded(q1[16:32, :] * weighted(ps, (), 16, 16, sf, -1))
        tail[...] = jnp.zeros((32, LANES), F32)
        tail[0:6, :] = ps[26:32, :]
        tail[6:8, :] = y1[30:32, :]
        for p in range(5):
            tail[8 + 2 * p : 10 + 2 * p, :] = x[p, 30:32, :]
        last_ref[:, lanes] = tail[...].astype(BF16)


def medium_spectrum(mf_ref, rate_ref, fwd_ref):
    lag = lax.broadcasted_iota(jnp.int32, (128, BLOCK), 0).astype(F32)
    damping = jnp.exp(-rate_ref[...] * lag) * (2.0 / POINTS)
    return damping, wide_dot(fwd_ref, slice(None), slice(0, 128), mf_ref[...] * damping)


def forward_kernel(
    se_ref,
    mr_ref,
    g_ref,
    before_ref,
    sw_ref,
    mw_ref,
    sf_ref,
    fwd_ref,
    feats,
    ps_ref,
    pb,
    own_d,
    x,
    ps,
    y1,
    tail,
    db,
):
    rows = se_ref.shape[1]
    for h in range(BLOCK // LANES):
        lanes = lanes_of(h)
        sw = feature_taps(sw_ref, lanes)
        mw = feature_taps(mw_ref, lanes)
        sf = short_taps(sf_ref, lanes)
        tail[...] = before_ref[:, lanes].astype(F32)
        ps[PAD - 6 : PAD, :] = tail[0:6, :]
        y1[PAD - 2 : PAD, :] = tail[6:8, :]
        for p in range(5):
            x[p, PAD - 2 : PAD, :] = tail[8 + 2 * p : 10 + 2 * p, :]
        for t, n in chunks(0, rows):
            for p in range(3):
                x[p, pl.ds(PAD + t, n), :] = se_ref[p, pl.ds(t, n), lanes].astype(F32)
            for p in range(2):
                x[3 + p, pl.ds(PAD + t, n), :] = mr_ref[p, pl.ds(t, n), lanes].astype(F32)
        for t, n in chunks(0, rows):
            r, at = PAD + t, pl.ds(t, n)
            key = weighted(x, (1,), r, n, sw[1], -1)
            value = weighted(x, (2,), r, n, sw[2], -1)
            product = (key * value).astype(BF16)
            ps_ref[at, lanes] = product
            ps[pl.ds(r, n), :] = product.astype(F32)
            query = weighted(x, (0,), r, n, sw[0], -1)
            feats[0, at, lanes] = query
            mixed = weighted(ps, (), r, n, sf, -1)
            feats[1, at, lanes] = mixed
            y1[pl.ds(r, n), :] = rounded(query * mixed)
            key = weighted(x, (4,), r, n, mw[1], -1)
            value = weighted(y1, (), r, n, mw[2], -1)
            feats[2, at, lanes] = key
            feats[3, at, lanes] = value
            pb[at, lanes] = (key * value).astype(BF16)
            query = weighted(x, (3,), r, n, mw[0], -1)
            high, low = split(g_ref[at, lanes].astype(F32) * query)
            db[0, at, lanes] = high
            db[1, at, lanes] = low
    own = slice(0, 256)
    own_d[...] = (
        dot(fwd_ref[0, :, own], db[0])
        + dot(fwd_ref[1, :, own], db[0])
        + dot(fwd_ref[0, :, own], db[1])
    )


def middle_kernel(
    norm_factor,
    feats,
    ps_ref,
    pb,
    own_d,
    mf_ref,
    rate_ref,
    before_ref,
    last_ref,
    ahead_ref,
    sw_ref,
    mw_ref,
    sf_ref,
    fwd_ref,
    inv_ref,
    medium_out,
    short_out,
    w2_out,
    dy1_out,
    feats_out,
    product_out,
    x,
    ps,
    y1,
    tail,
    db,
    d,
    dz,
):
    rows = feats.shape[1]
    top = lax.broadcasted_iota(jnp.int32, (REACH, LANES), 0) < 2
    here = pl.ds(PAD, REACH)
    for h in range(BLOCK // LANES):
        lanes = lanes_of(h)
        sw = feature_taps(sw_ref, lanes)
        mw = feature_taps(mw_ref, lanes)
        sf = short_taps(sf_ref, lanes)
        tail[...] = last_ref[:, lanes].astype(F32)
        ps[PAD - 6 : PAD, :] = tail[0:6, :]
        y1[PAD - 2 : PAD, :] = tail[6:8, :]
        for p in range(5):
            x[p, PAD - 2 : PAD, :] = tail[8 + 2 * p : 10 + 2 * p, :]
            x[p, here, :] = jnp.zeros((REACH, LANES), F32)
        tail[...] = ahead_ref[144:176, lanes].astype(F32)
        x[3, PAD : PAD + 2, :] = tail[2:4, :]
        x[4, PAD : PAD + 10, :] = tail[4:14, :]
        x[0, PAD : PAD + 8, :] = tail[14:22, :]
        x[1, PAD : PAD + 2, :] = tail[22:24, :]
        x[2, PAD : PAD + 2, :] = tail[24:26, :]
        query = weighted(x, (0,), PAD, REACH, sw[0], -1)
        key = weighted(x, (1,), PAD, REACH, sw[1], -1)
        value = weighted(x, (2,), PAD, REACH, sw[2], -1)
        feats_out[0, :, lanes] = query
        feats_out[4, :, lanes] = key
        feats_out[5, :, lanes] = value
        ps[here, :] = rounded(key * value)
        mixed = weighted(ps, (), PAD, REACH, sf, -1)
        feats_out[1, :, lanes] = mixed
        y1[here, :] = rounded(query * mixed)
        key = weighted(x, (4,), PAD, REACH, mw[1], -1)
        value = weighted(y1, (), PAD, REACH, mw[2], -1)
        feats_out[2, :, lanes] = key
        feats_out[3, :, lanes] = value
        product_out[:, lanes] = jnp.where(top, key * value, 0.0).astype(BF16)
        upstream = tail[0:REACH, :] * weighted(x, (3,), PAD, REACH, mw[0], -1)
        upstream = jnp.where(top, upstream, ahead_ref[0:REACH, lanes].astype(F32))
        db[0:REACH, lanes] = upstream.astype(BF16)
        db[REACH : POINTS - 256, lanes] = ahead_ref[REACH : POINTS - 256, lanes]
        db[POINTS - 256 : 256, lanes] = jnp.zeros((DEPTH - POINTS, LANES), BF16)

    beyond = slice(256, DEPTH)
    damping, kernel = medium_spectrum(mf_ref, rate_ref, fwd_ref)
    own = slice(0, 256)
    pp = dot(fwd_ref[0, :, own], pb[...]) + dot(fwd_ref[1, :, own], pb[...])
    dd = own_d[...] + (dot(fwd_ref[0, :, beyond], db[...]) + dot(fwd_ref[1, :, beyond], db[...]))
    spread = wide_dot(inv_ref, slice(None), slice(None), product_of(kernel, dd, True))
    w2_out[...] = spread
    lagged = wide_dot(inv_ref, slice(0, 128), slice(None), product_of(pp, dd, True))
    medium_out[...] = (lagged * (damping * norm_factor)).astype(BF16)

    for h in range(BLOCK // LANES):
        lanes = lanes_of(h)
        mw = feature_taps(mw_ref, lanes)
        tail[...] = before_ref[:, lanes].astype(F32)
        ps[PAD - 6 : PAD, :] = tail[0:6, :]
        for t, n in chunks(0, rows):
            at = pl.ds(t, n)
            ps[pl.ds(PAD + t, n), :] = ps_ref[at, lanes].astype(F32)
            d[at, :] = w2_out[at, lanes] * feats[2, at, lanes]
        last = pl.ds(rows, REACH)
        d[last, :] = w2_out[last, lanes] * feats_out[2, :, lanes]
        d[rows + REACH : rows + REACH + 8, :] = jnp.zeros((8, LANES), F32)
        dy1_out[last, lanes] = weighted(d, (), rows, REACH, mw[2], 1)
        sums = [jnp.zeros((8, LANES), F32) for _ in range(7)]
        for t, n in chunks(0, rows):
            at = pl.ds(t, n)
            grad = weighted(d, (), t, n, mw[2], 1)
            dy1_out[at, lanes] = grad
            grad = grad * feats[0, at, lanes]
            for j in range(7):
                term = grad * ps[pl.ds(PAD + t - j, n), :]
                sums[j] = sums[j] + jnp.sum(term.reshape(n // 8, 8, LANES), axis=0)
        for j in range(7):
            tail[j : j + 1, :] = jnp.sum(sums[j], axis=0, keepdims=True)
        tail[7:8, :] = jnp.zeros((1, LANES), F32)
        short_out[:, lanes] = tail[0:8, :] * norm_factor


def backward_kernel(
    feats,
    feats_ahead,
    w2,
    dy1,
    own_ref,
    mf_ref,
    rate_ref,
    behind_ref,
    product_ref,
    se_ref,
    before_ref,
    g_ref,
    ahead_ref,
    sw_ref,
    mw_ref,
    sf_ref,
    fwd_ref,
    rim_ref,
    inv_ref,
    se_out,
    mr_out,
    x,
    pb,
    z2,
    tail,
    d,
    e,
    dz,
):
    rows = feats.shape[1]
    pb[0:128, :] = behind_ref[...]
    pb[128 : 128 + REACH, :] = product_ref[...]
    pb[128 + REACH : 256, :] = jnp.zeros((128 - REACH, BLOCK), BF16)
    _, kernel = medium_spectrum(mf_ref, rate_ref, fwd_ref)
    own = slice(0, 256)
    pp = (
        dot(fwd_ref[0, :, own], own_ref[...])
        + dot(fwd_ref[1, :, own], own_ref[...])
        + dot(rim_ref[0], pb[...])
        + dot(rim_ref[1], pb[...])
    )
    z2[...] = wide_dot(inv_ref, slice(None), slice(None), product_of(kernel, pp, False))
    spans = [(feats, 0, t, n) for t, n in chunks(0, rows)] + [(feats_ahead, rows, rows, REACH)]
    for h in range(BLOCK // LANES):
        lanes = lanes_of(h)
        sw = feature_taps(sw_ref, lanes)
        mw = feature_taps(mw_ref, lanes)
        sf = short_taps(sf_ref, lanes)
        tail[...] = before_ref[:, lanes].astype(F32)
        for p in range(2):
            x[p, PAD - 2 : PAD, :] = tail[10 + 2 * p : 12 + 2 * p, :]
            for t, n in chunks(0, rows):
                x[p, pl.ds(PAD + t, n), :] = se_ref[1 + p, pl.ds(t, n), lanes].astype(F32)
        tail[...] = ahead_ref[144:176, lanes].astype(F32)
        tail[2:16, :] = jnp.zeros((14, LANES), F32)
        for source, base, t, n in spans:
            at, own = pl.ds(t, n), pl.ds(t - base, n)
            grad = w2[at, lanes]
            d[1, at, :] = grad * source[3, own, lanes]
            upstream = tail[0:REACH, :] if base else g_ref[at, lanes].astype(F32)
            d[0, at, :] = upstream * z2[at, lanes]
            grad = dy1[at, lanes]
            e[0, at, :] = grad * source[1, own, lanes]
            dz[at, :] = grad * source[0, own, lanes]
        for source, base, t, n in spans:
            at, own = pl.ds(t, n), pl.ds(t - base, n)
            grad = weighted(dz, (), t, n, sf, 1)
            if base:
                key, value = source[4, own, lanes], source[5, own, lanes]
            else:
                key = weighted(x, (0,), PAD + t, n, sw[1], -1)
                value = weighted(x, (1,), PAD + t, n, sw[2], -1)
            e[1, at, :] = grad * value
            e[2, at, :] = grad * key
        for t, n in chunks(0, rows):
            at = pl.ds(t, n)
            for p in range(2):
                mr_out[p, at, lanes] = weighted(d, (p,), t, n, mw[p], 1).astype(BF16)
            for p in range(3):
                se_out[p, at, lanes] = weighted(e, (p,), t, n, sw[p], 1).astype(BF16)


def rows_of(*dims):
    return pl.BlockSpec(dims + (BLOCK,), lambda i: (0,) * len(dims) + (i,))


def fixed(array):
    return pl.BlockSpec(array.shape, lambda i: (0,) * array.ndim)


def f32_rows(*dims):
    return pltpu.VMEM(dims + (LANES,), F32)


def bf16_rows(*dims):
    return pltpu.VMEM(dims + (BLOCK,), BF16)


def blocks_call(name, body, arrays, tables, outs, scratch, flops):
    channels = arrays[0].shape[-1]
    return pl.pallas_call(
        body,
        grid=(channels // BLOCK,),
        in_specs=[rows_of(*a.shape[:-1]) for a in arrays] + [fixed(t) for t in tables],
        out_specs=[rows_of(*dims) for dims, _ in outs],
        out_shape=[jax.ShapeDtypeStruct(dims + (channels,), kind) for dims, kind in outs],
        scratch_shapes=scratch,
        compiler_params=pltpu.CompilerParams(vmem_limit_bytes=56 * 2**20),
        cost_estimate=pl.CostEstimate(
            flops=flops * 256 * channels, bytes_accessed=16 * 256 * channels, transcendentals=0
        ),
        name=name,
    )(*arrays, *tables)


def edges(se, mr, g, sw, mw, sf):
    rows, channels = g.shape
    wide = min(channels, 512)

    def part(lead, count, at):
        zeros = (0,) * len(lead)
        return pl.BlockSpec(lead + (count, wide), lambda i: zeros + (at, i))

    return pl.pallas_call(
        edge_kernel,
        grid=(channels // wide,),
        in_specs=[
            part((3,), 16, 0),
            part((3,), 32, rows // 32 - 1),
            part((2,), 144, 0),
            part((2,), 32, rows // 32 - 1),
            part((), 144, 0),
            part((3,), 3, 0),
            part((3,), 3, 0),
            part((), 7, 0),
        ],
        out_specs=[part((), 32, 0), part((), 176, 0)],
        out_shape=[
            jax.ShapeDtypeStruct((32, channels), BF16),
            jax.ShapeDtypeStruct((176, channels), BF16),
        ],
        scratch_shapes=[
            f32_rows(5, 160),
            f32_rows(32),
            f32_rows(32),
            f32_rows(32),
            f32_rows(32),
        ],
        compiler_params=pltpu.CompilerParams(vmem_limit_bytes=56 * 2**20),
        name="edges",
    )(se, se, mr, mr, g, sw, mw, sf)


def ctx_sums(short_rows, medium_part):
    count = lax.axis_size("ctx")
    channels = short_rows.shape[1]
    medium_length = medium_part.shape[0]
    depth = medium_length // count
    width = short_rows.size // (count * depth)
    terms = jnp.concatenate(
        [
            medium_part.reshape(count, depth, channels),
            short_rows.astype(BF16).reshape(count, depth, width),
        ],
        axis=2,
    )
    shares = lax.all_to_all(terms, "ctx", 0, 0, tiled=True)
    total = jnp.sum(shares.astype(F32), axis=0).astype(BF16)
    copies = jnp.broadcast_to(total[None], (count,) + total.shape)
    totals = lax.all_to_all(copies, "ctx", 0, 0, tiled=True).astype(F32)
    medium_total = totals[:, :, :channels].reshape(medium_length, channels)
    short_total = totals[:, :, channels:].reshape(short_rows.shape)[:7]
    return short_total, medium_total


def local(tables, se_input, mr_input, g, sw, mw, sf, mf, decay_rate):
    rows, channels = g.shape
    end = rows + REACH
    count = lax.axis_size("ctx")
    norm_factor = 1.0 / math.sqrt(rows * count)
    fwd, rim, inv = (jnp.asarray(table) for table in tables)
    se = jnp.transpose(se_input, (1, 0, 2))
    mr = jnp.transpose(mr_input, (1, 0, 2))
    onward = [(i, i + 1) for i in range(count - 1)]
    backward = [(i, i - 1) for i in range(1, count)]
    rate = decay_rate[None, :]

    last, first = edges(se, mr, g, sw, mw, sf)
    before = lax.ppermute(last, "ctx", onward)
    ahead = lax.ppermute(first, "ctx", backward)
    feats, ps, product, own_d = blocks_call(
        "forward",
        forward_kernel,
        [se, mr, g, before, sw, mw, sf],
        [fwd],
        [
            ((4, rows), F32),
            ((rows,), BF16),
            ((rows,), BF16),
            ((POINTS,), F32),
        ],
        [
            f32_rows(5, PAD + rows),
            f32_rows(PAD + rows),
            f32_rows(PAD + rows),
            f32_rows(32),
            bf16_rows(2, rows),
        ],
        4000,
    )
    behind = lax.ppermute(product[rows - 128 :], "ctx", onward)
    medium_part, short_rows, w2, dy1, feats_ahead, product_ahead = blocks_call(
        "middle",
        functools.partial(middle_kernel, norm_factor),
        [feats, ps, product, own_d, mf, rate, before, last, ahead, sw, mw, sf],
        [fwd, inv],
        [
            ((128,), BF16),
            ((8,), F32),
            ((end,), F32),
            ((end,), F32),
            ((6, REACH), F32),
            ((REACH,), BF16),
        ],
        [
            f32_rows(5, 32),
            f32_rows(PAD + rows),
            f32_rows(32),
            f32_rows(32),
            bf16_rows(256),
            f32_rows(end + 16),
            f32_rows(end + 16),
        ],
        4000,
    )
    medium_part, behind = lax.optimization_barrier((medium_part, behind))
    se_out, mr_out = blocks_call(
        "backward",
        backward_kernel,
        [
            feats,
            feats_ahead,
            w2,
            dy1,
            product,
            mf,
            rate,
            behind,
            product_ahead,
            se,
            before,
            g,
            ahead,
            sw,
            mw,
            sf,
        ],
        [fwd, rim, inv],
        [((3, rows), BF16), ((2, rows), BF16)],
        [
            f32_rows(2, PAD + rows),
            bf16_rows(256),
            pltpu.VMEM((end, BLOCK), F32),
            f32_rows(32),
            f32_rows(2, end + 16),
            f32_rows(3, end + 16),
            f32_rows(end + 16),
        ],
        4000,
    )
    short_total, medium_total = ctx_sums(short_rows, medium_part)
    return (
        jnp.transpose(se_out, (1, 0, 2)),
        jnp.transpose(mr_out, (1, 0, 2)),
        short_total,
        medium_total,
    )


def solution(mesh):
    tables = transform_tables()
    placed = (
        P("ctx", None, "ts"),
        P("ctx", None, "ts"),
        P("ctx", "ts"),
        P(None, None, "ts"),
        P(None, None, "ts"),
        P(None, "ts"),
        P(None, "ts"),
        P("ts"),
    )
    return jax.shard_map(
        functools.partial(local, tables),
        mesh=mesh,
        in_specs=placed,
        out_specs=(P("ctx", None, "ts"), P("ctx", None, "ts"), P(None, "ts"), P(None, "ts")),
        check_vma=False,
    )
```

profile of v0, /device:TPU:16, one launch (start us, length us, event | category | flops | bytes accessed | tf_op | source)
XLA Modules:
  0.0 92.3 jit_solution(14586506686397854386)
XLA Ops:
  0.6 2.5 %copy.18 = bf16[256,2,1024]{2,0,1:T(8,128)(2,1)} copy(bf16[256,2,1024]{2,1,0:T(2,128)(2,1)} %param.12) | data formatting | bytes 2097152 | tf_op args[1]
  3.1 2.3 %edges.1 = (bf16[32,1024]{1,0:T(8,128)(2,1)}, bf16[176,1024]{1,0:T(8,128)(2,1)}) custom-call(bf16[3,256,1024]{2,1,0:T(8,128)(2,1)} %bitcast.7, bf16[3,256,1024]{2,1,0:T(8,128)(2,1)} %bitcast.8, bf16[2,256,1024]{2,1,0:T(8,128)(2,1)} %bitcast.11, bf16[2,256,1024]{2,1,0:T(8,128)(2,1)} %bitcast.12, bf16[256,1024]{1,0:T(8,128)(2,1)} %g_ref.5, ...), custom_call_target="tpu_custom_call" | custom-call | tf_op jit(solution)/shard_map/edges/pallas_call | solution.py:446
  5.4 1.3 %collective-permute-start.1 = (bf16[176,1024]{1,0:T(8,128)(2,1)}, bf16[176,1024]{1,0:T(8,128)(2,1)S(1)}, u32[]{:S(2)}, u32[]{:S(2)}) collective-permute-start(bf16[176,1024]{1,0:T(8,128)(2,1)} %get-tuple-element.25), channel_id=1, source_target_pairs={{4,0},{8,4},{12,8},{16,12},{20,16},{24,20},{28,24},{32,28},{36,32}... | collective-permute-start | bytes 1081352 | tf_op jit(solution)/shard_map/ppermute | solution.py:512
  6.7 4.5 %collective-permute-start = (bf16[32,1024]{1,0:T(8,128)(2,1)}, bf16[32,1024]{1,0:T(8,128)(2,1)S(1)}, u32[]{:S(2)}, u32[]{:S(2)}) collective-permute-start(bf16[32,1024]{1,0:T(8,128)(2,1)} %get-tuple-element.20.last_ref), channel_id=1, source_target_pairs={{0,4},{4,8},{8,12},{12,16},{16,20},{20,24},{24,28},{28,32},{32,36}... | collective-permute-start | bytes 196616 | tf_op jit(solution)/shard_map/ppermute | solution.py:511
  11.2 7.6 %collective-permute-done.before_ref = bf16[32,1024]{1,0:T(8,128)(2,1)S(1)} collective-permute-done((bf16[32,1024]{1,0:T(8,128)(2,1)}, bf16[32,1024]{1,0:T(8,128)(2,1)S(1)}, u32[]{:S(2)}, u32[]{:S(2)}) %collective-permute-start) | collective-permute-done | bytes 65568 | tf_op jit(solution)/shard_map/ppermute | solution.py:511
  18.8 0.0 copy-start.1
  18.8 0.6 copy-done.1
  19.5 6.9 %forward.1 = (f32[4,256,1024]{2,1,0:T(8,128)}, bf16[256,1024]{1,0:T(8,128)(2,1)}, bf16[256,1024]{1,0:T(8,128)(2,1)}, f32[400,1024]{1,0:T(8,128)}) custom-call(bf16[3,256,1024]{2,1,0:T(8,128)(2,1)} %bitcast.9, bf16[2,256,1024]{2,1,0:T(8,128)(2,1)} %bitcast.13, bf16[256,1024]{1,0:T(8,128)(2,1)} %g_ref.5, bf16[32,1024]{1,0:T(8,128)(2,1)} %copy-done.1, ...), custom_call_target="tpu_custom_call" | custom-call | flops 1048576000 | bytes 4194304 | tf_op jit(solution)/shard_map/forward/pallas_call | solution.py:423
  26.3 1.0 %slice.14 = bf16[128,1024]{1,0:T(8,128)(2,1)S(1)} slice(bf16[256,1024]{1,0:T(8,128)(2,1)} %get-tuple-element.23.pb.own_ref), slice={[128:256], [0:1024]} | slice | bytes 524288 | tf_op jit(solution)/shard_map/slice | solution.py:533
  27.3 4.3 %collective-permute-start.2 = (bf16[128,1024]{1,0:T(8,128)(2,1)S(1)}, bf16[128,1024]{1,0:T(8,128)(2,1)S(1)}, u32[]{:S(2)}, u32[]{:S(2)}) collective-permute-start(bf16[128,1024]{1,0:T(8,128)(2,1)S(1)} %slice.14), channel_id=1, source_target_pairs={{0,4},{4,8},{8,12},{12,16},{16,20},{20,24},{24,28},{28,32},{32,36}... | collective-permute-start | bytes 786440 | tf_op jit(solution)/shard_map/ppermute | solution.py:533
  31.6 0.0 collective-permute-done.1.ahead_ref
  31.6 0.0 copy-start
  31.6 0.8 copy-done
  32.4 9.8 %middle.1 = (bf16[128,1024]{1,0:T(8,128)(2,1)}, f32[8,1024]{1,0:T(8,128)}, f32[272,1024]{1,0:T(8,128)}, f32[272,1024]{1,0:T(8,128)}, f32[6,16,1024]{2,1,0:T(8,128)}, /*index=5*/bf16[16,1024]{1,0:T(8,128)(2,1)}) custom-call(f32[4,256,1024]{2,1,0:T(8,128)} %get-tuple-element.21.feats, bf16[256,1024]{1,0:T(8,128)(2,1)} %get-tuple-element.22.ps_ref, ...), custom_call_target="tpu_custom_call" | custom-call | flops 1048576000 | bytes 4194304 | tf_op jit(solution)/shard_map/middle/pallas_call | solution.py:423
  42.2 0.0 collective-permute-done.2.behind_ref
  42.2 0.0 copy-start.2
  42.2 0.8 convert_element_type.8
  43.0 0.1 reshape.21
  43.1 1.1 %reshape.20 = bf16[64,2,1024]{2,1,0:T(2,128)(2,1)S(1)} reshape(bf16[128,1024]{1,0:T(8,128)(2,1)} %get-tuple-element.34) | data formatting | bytes 524288 | tf_op jit(solution)/shard_map/reshape | solution.py:484
  44.2 0.3 pad_maximum_fusion
  44.4 24.5 %all_to_all.10 = bf16[64,2,1088]{2,1,0:T(2,128)(2,1)S(1)} all-to-all(bf16[64,2,1088]{2,1,0:T(2,128)(2,1)S(1)} %pad_maximum_fusion), channel_id=1, replica_groups=mesh['ctx'=64,'ts'=4] {'ctx'}, dimensions={0} | all-to-all | bytes 557056 | tf_op jit(solution)/shard_map/all_to_all | solution.py:489
  68.9 0.3 reduce_sum.12
  69.2 0.9 broadcast_in_dim.10
  70.1 5.9 %all-to-all-start.1 = ((bf16[64,2,1088]{2,1,0:T(2,128)(2,1)}), bf16[64,2,1088]{2,1,0:T(2,128)(2,1)S(1)}, u32[]{:S(2)}, u32[]{:S(2)}) async-start(bf16[64,2,1088]{2,1,0:T(2,128)(2,1)} %broadcast_in_dim.10), calls=%async_computation.1 | async-start | bytes 589824 | tf_op jit(solution)/shard_map/all_to_all | solution.py:492
  76.0 0.0 copy-done.2
  76.0 10.9 %backward.1 = (bf16[3,256,1024]{2,1,0:T(8,128)(2,1)}, bf16[2,256,1024]{2,1,0:T(8,128)(2,1)}) custom-call(f32[4,256,1024]{2,1,0:T(8,128)} %get-tuple-element.21.feats, f32[6,16,1024]{2,1,0:T(8,128)} %get-tuple-element.26.feats_ahead, f32[272,1024]{1,0:T(8,128)} %get-tuple-element.27.w2, f32[272,1024]{1,0:T(8,128)} %get-tuple-element.28.dy1, ...), custom_call_target="tpu_custom_call" | custom-call | flops 1048576000 | bytes 4194304 | tf_op jit(solution)/shard_map/backward/pallas_call | solution.py:423
  86.9 3.3 %copy.16 = bf16[256,2,1024]{2,1,0:T(2,128)(2,1)} copy(bf16[256,2,1024]{2,0,1:T(8,128)(2,1)} %bitcast.14) | data formatting | bytes 2097152
  90.2 0.0 all-to-all-done.1
  90.2 0.7 slice.16
  90.9 0.2 slice.19
  91.1 1.2 %reshape.22 = f32[128,1024]{1,0:T(8,128)} reshape(f32[64,2,1024]{2,1,0:T(2,128)S(1)} %slice.19) | data formatting | bytes 1048576 | tf_op jit(solution)/shard_map/reshape | solution.py:493
  (1 shorter events, 0.0 us)
Async XLA Ops:
  5.4 26.2 %collective-permute-start.1 = (bf16[176,1024]{1,0:T(8,128)(2,1)}, bf16[176,1024]{1,0:T(8,128)(2,1)S(1)}, u32[]{:S(2)}, u32[]{:S(2)}) collective-permute-start(bf16[176,1024]{1,0:T(8,128)(2,1)} %get-tuple-element.25), channel_id=1, source_target_pairs={{4,0},{8,4},{12,8},{16,12},{20,16},{24,20},{28,24},{32,28},{36,32}... | collective-permute-start | bytes 1081352 | tf_op jit(solution)/shard_map/ppermute | solution.py:512
  6.7 12.2 %collective-permute-start = (bf16[32,1024]{1,0:T(8,128)(2,1)}, bf16[32,1024]{1,0:T(8,128)(2,1)S(1)}, u32[]{:S(2)}, u32[]{:S(2)}) collective-permute-start(bf16[32,1024]{1,0:T(8,128)(2,1)} %get-tuple-element.20.last_ref), channel_id=1, source_target_pairs={{0,4},{4,8},{8,12},{12,16},{16,20},{20,24},{24,28},{28,32},{32,36}... | collective-permute-start | bytes 196616 | tf_op jit(solution)/shard_map/ppermute | solution.py:511
  18.8 0.6 copy-start.1
  27.3 14.9 %collective-permute-start.2 = (bf16[128,1024]{1,0:T(8,128)(2,1)S(1)}, bf16[128,1024]{1,0:T(8,128)(2,1)S(1)}, u32[]{:S(2)}, u32[]{:S(2)}) collective-permute-start(bf16[128,1024]{1,0:T(8,128)(2,1)S(1)} %slice.14), channel_id=1, source_target_pairs={{0,4},{4,8},{8,12},{12,16},{16,20},{20,24},{24,28},{28,32},{32,36}... | collective-permute-start | bytes 786440 | tf_op jit(solution)/shard_map/ppermute | solution.py:533
  31.6 0.8 copy-start
  42.2 33.8 %copy-start.2 = (bf16[128,1024]{1,0:T(8,128)(2,1)}, bf16[128,1024]{1,0:T(8,128)(2,1)S(1)}, u32[]{:S(2)}) copy-start(bf16[128,1024]{1,0:T(8,128)(2,1)S(1)} %collective-permute-done.2.behind_ref) | copy-start | bytes 786436
  70.1 20.1 %all-to-all-start.1 = ((bf16[64,2,1088]{2,1,0:T(2,128)(2,1)}), bf16[64,2,1088]{2,1,0:T(2,128)(2,1)S(1)}, u32[]{:S(2)}, u32[]{:S(2)}) async-start(bf16[64,2,1088]{2,1,0:T(2,128)(2,1)} %broadcast_in_dim.10), calls=%async_computation.1 | async-start | bytes 589824 | tf_op jit(solution)/shard_map/all_to_all | solution.py:492
where the time goes:
time: 93.5 us; the launch traced here: 92.3 us
  Pallas kernels  29.9 us (32%)
  blocking collectives  24.5 us (26%)
  starting transfers between devices  16 us (17%)
  local copies, waits for them, and re-layouts  12.2 us (13%)
  waiting for transfers between devices  7.62 us (8%)
  other arithmetic  1.34 us (1%)
    pallas_call x3, Pallas kernels, blocks_call(): pl.pallas_call(body, grid=(channels // BLOCK,), in_specs=[rows_of(*a.shap...  27.6 us
    all_to_all x1, blocking collectives, ctx_sums(): shares = lax.all_to_all(terms, 'ctx', 0, 0, tiled=True)  24.5 us
    ppermute x1, waiting for transfers between devices, local(): before = lax.ppermute(last, 'ctx', onward)  7.61 us
    unnamed x8, local copies, waits for them, and re-layouts  7.11 us
    all_to_all x1, starting transfers between devices, ctx_sums(): totals = lax.all_to_all(copies, 'ctx', 0, 0, tiled=True).astype(F32)  5.86 us
    ppermute x1, starting transfers between devices, local(): before = lax.ppermute(last, 'ctx', onward)  4.55 us
    ppermute x1, starting transfers between devices, local(): behind = lax.ppermute(product[rows - 128:], 'ctx', onward)  4.3 us
    pallas_call x1, Pallas kernels, edges(): pl.pallas_call(edge_kernel, grid=(channels // wide,), in_specs=[part((3,)...  2.28 us
  transfers between devices with their start and end apart: 4, of which 1 were waited for; matrix products, arithmetic and copies ran while one was open for 5% of the time, Pallas kernels for 30%

commit v1 on v0

--- a/solution.py
+++ b/solution.py
@@ -155,7 +155,10 @@
     mw_ref,
     sf_ref,
     fwd_ref,
-    feats,
+    q1_ref,
+    z1_ref,
+    k2_ref,
+    v2_ref,
     ps_ref,
     pb,
     own_d,
@@ -189,14 +192,14 @@
             ps_ref[at, lanes] = product
             ps[pl.ds(r, n), :] = product.astype(F32)
             query = weighted(x, (0,), r, n, sw[0], -1)
-            feats[0, at, lanes] = query
+            q1_ref[at, lanes] = query
             mixed = weighted(ps, (), r, n, sf, -1)
-            feats[1, at, lanes] = mixed
+            z1_ref[at, lanes] = mixed
             y1[pl.ds(r, n), :] = rounded(query * mixed)
             key = weighted(x, (4,), r, n, mw[1], -1)
             value = weighted(y1, (), r, n, mw[2], -1)
-            feats[2, at, lanes] = key
-            feats[3, at, lanes] = value
+            k2_ref[at, lanes] = key
+            v2_ref[at, lanes] = value
             pb[at, lanes] = (key * value).astype(BF16)
             query = weighted(x, (3,), r, n, mw[0], -1)
             high, low = split(g_ref[at, lanes].astype(F32) * query)
@@ -212,7 +215,8 @@
 
 def middle_kernel(
     norm_factor,
-    feats,
+    q1_ref,
+    k2_ref,
     ps_ref,
     pb,
     own_d,
@@ -231,6 +235,7 @@
     w2_out,
     dy1_out,
     feats_out,
+    v2_out,
     product_out,
     x,
     ps,
@@ -240,7 +245,7 @@
     d,
     dz,
 ):
-    rows = feats.shape[1]
+    rows = q1_ref.shape[0]
     top = lax.broadcasted_iota(jnp.int32, (REACH, LANES), 0) < 2
     here = pl.ds(PAD, REACH)
     for h in range(BLOCK // LANES):
@@ -264,8 +269,8 @@
         key = weighted(x, (1,), PAD, REACH, sw[1], -1)
         value = weighted(x, (2,), PAD, REACH, sw[2], -1)
         feats_out[0, :, lanes] = query
-        feats_out[4, :, lanes] = key
-        feats_out[5, :, lanes] = value
+        feats_out[3, :, lanes] = key
+        feats_out[4, :, lanes] = value
         ps[here, :] = rounded(key * value)
         mixed = weighted(ps, (), PAD, REACH, sf, -1)
         feats_out[1, :, lanes] = mixed
@@ -273,7 +278,7 @@
         key = weighted(x, (4,), PAD, REACH, mw[1], -1)
         value = weighted(y1, (), PAD, REACH, mw[2], -1)
         feats_out[2, :, lanes] = key
-        feats_out[3, :, lanes] = value
+        v2_out[:, lanes] = value
         product_out[:, lanes] = jnp.where(top, key * value, 0.0).astype(BF16)
         upstream = tail[0:REACH, :] * weighted(x, (3,), PAD, REACH, mw[0], -1)
         upstream = jnp.where(top, upstream, ahead_ref[0:REACH, lanes].astype(F32))
@@ -299,7 +304,7 @@
         for t, n in chunks(0, rows):
             at = pl.ds(t, n)
             ps[pl.ds(PAD + t, n), :] = ps_ref[at, lanes].astype(F32)
-            d[at, :] = w2_out[at, lanes] * feats[2, at, lanes]
+            d[at, :] = w2_out[at, lanes] * k2_ref[at, lanes]
         last = pl.ds(rows, REACH)
         d[last, :] = w2_out[last, lanes] * feats_out[2, :, lanes]
         d[rows + REACH : rows + REACH + 8, :] = jnp.zeros((8, LANES), F32)
@@ -309,47 +314,78 @@
             at = pl.ds(t, n)
             grad = weighted(d, (), t, n, mw[2], 1)
             dy1_out[at, lanes] = grad
-            grad = grad * feats[0, at, lanes]
+            grad = grad * q1_ref[at, lanes]
             for j in range(7):
                 term = grad * ps[pl.ds(PAD + t - j, n), :]
                 sums[j] = sums[j] + jnp.sum(term.reshape(n // 8, 8, LANES), axis=0)
         for j in range(7):
             tail[j : j + 1, :] = jnp.sum(sums[j], axis=0, keepdims=True)
         tail[7:8, :] = jnp.zeros((1, LANES), F32)
-        short_out[:, lanes] = tail[0:8, :] * norm_factor
-
-
-def backward_kernel(
-    feats,
-    feats_ahead,
+        short_out[:, lanes] = (tail[0:16, :] * norm_factor).astype(BF16)[0:8]
+
+
+def spans(rows):
+    return [(0, t, n) for t, n in chunks(0, rows)] + [(rows, rows, REACH)]
+
+
+def se_backward_kernel(
+    q1_ref, z1_ref, feats_ahead, dy1, se_ref, before_ref, sw_ref, sf_ref, se_out, x, tail, e, dz
+):
+    rows = q1_ref.shape[0]
+    for h in range(BLOCK // LANES):
+        lanes = lanes_of(h)
+        sw = feature_taps(sw_ref, lanes)
+        sf = short_taps(sf_ref, lanes)
+        tail[...] = before_ref[:, lanes].astype(F32)
+        for p in range(2):
+            x[p, PAD - 2 : PAD, :] = tail[10 + 2 * p : 12 + 2 * p, :]
+            for t, n in chunks(0, rows):
+                x[p, pl.ds(PAD + t, n), :] = se_ref[1 + p, pl.ds(t, n), lanes].astype(F32)
+        for base, t, n in spans(rows):
+            at, own = pl.ds(t, n), pl.ds(t - base, n)
+            grad = dy1[at, lanes]
+            query = feats_ahead[0, own, lanes] if base else q1_ref[own, lanes]
+            mixed = feats_ahead[1, own, lanes] if base else z1_ref[own, lanes]
+            e[0, at, :] = grad * mixed
+            dz[at, :] = grad * query
+        for base, t, n in spans(rows):
+            at, own = pl.ds(t, n), pl.ds(t - base, n)
+            grad = weighted(dz, (), t, n, sf, 1)
+            if base:
+                key, value = feats_ahead[3, own, lanes], feats_ahead[4, own, lanes]
+            else:
+                key = weighted(x, (0,), PAD + t, n, sw[1], -1)
+                value = weighted(x, (1,), PAD + t, n, sw[2], -1)
+            e[1, at, :] = grad * value
+            e[2, at, :] = grad * key
+        for t, n in chunks(0, rows):
+            at = pl.ds(t, n)
+            for p in range(3):
+                se_out[p, at, lanes] = weighted(e, (p,), t, n, sw[p], 1).astype(BF16)
+
+
+def mr_backward_kernel(
+    v2,
+    v2_ahead,
     w2,
-    dy1,
     own_ref,
     mf_ref,
     rate_ref,
     behind_ref,
     product_ref,
-    se_ref,
-    before_ref,
     g_ref,
     ahead_ref,
-    sw_ref,
     mw_ref,
-    sf_ref,
     fwd_ref,
     rim_ref,
     inv_ref,
-    se_out,
     mr_out,
-    x,
     pb,
     z2,
     tail,
     d,
-    e,
-    dz,
 ):
-    rows = feats.shape[1]
+    rows = v2.shape[0]
     pb[0:128, :] = behind_ref[...]
     pb[128 : 128 + REACH, :] = product_ref[...]
     pb[128 + REACH : 256, :] = jnp.zeros((128 - REACH, BLOCK), BF16)
@@ -362,44 +398,20 @@
         + dot(rim_ref[1], pb[...])
     )
     z2[...] = wide_dot(inv_ref, slice(None), slice(None), product_of(kernel, pp, False))
-    spans = [(feats, 0, t, n) for t, n in chunks(0, rows)] + [(feats_ahead, rows, rows, REACH)]
     for h in range(BLOCK // LANES):
         lanes = lanes_of(h)
-        sw = feature_taps(sw_ref, lanes)
         mw = feature_taps(mw_ref, lanes)
-        sf = short_taps(sf_ref, lanes)
-        tail[...] = before_ref[:, lanes].astype(F32)
-        for p in range(2):
-            x[p, PAD - 2 : PAD, :] = tail[10 + 2 * p : 12 + 2 * p, :]
-            for t, n in chunks(0, rows):
-                x[p, pl.ds(PAD + t, n), :] = se_ref[1 + p, pl.ds(t, n), lanes].astype(F32)
         tail[...] = ahead_ref[144:176, lanes].astype(F32)
         tail[2:16, :] = jnp.zeros((14, LANES), F32)
-        for source, base, t, n in spans:
+        for base, t, n in spans(rows):
             at, own = pl.ds(t, n), pl.ds(t - base, n)
-            grad = w2[at, lanes]
-            d[1, at, :] = grad * source[3, own, lanes]
+            value = v2_ahead[own, lanes] if base else v2[own, lanes]
+            d[1, at, :] = w2[at, lanes] * value
             upstream = tail[0:REACH, :] if base else g_ref[at, lanes].astype(F32)
             d[0, at, :] = upstream * z2[at, lanes]
-            grad = dy1[at, lanes]
-            e[0, at, :] = grad * source[1, own, lanes]
-            dz[at, :] = grad * source[0, own, lanes]
-        for source, base, t, n in spans:
-            at, own = pl.ds(t, n), pl.ds(t - base, n)
-            grad = weighted(dz, (), t, n, sf, 1)
-            if base:
-                key, value = source[4, own, lanes], source[5, own, lanes]
-            else:
-                key = weighted(x, (0,), PAD + t, n, sw[1], -1)
-                value = weighted(x, (1,), PAD + t, n, sw[2], -1)
-            e[1, at, :] = grad * value
-            e[2, at, :] = grad * key
         for t, n in chunks(0, rows):
-            at = pl.ds(t, n)
             for p in range(2):
-                mr_out[p, at, lanes] = weighted(d, (p,), t, n, mw[p], 1).astype(BF16)
-            for p in range(3):
-                se_out[p, at, lanes] = weighted(e, (p,), t, n, sw[p], 1).astype(BF16)
+                mr_out[p, pl.ds(t, n), lanes] = weighted(d, (p,), t, n, mw[p], 1).astype(BF16)
 
 
 def rows_of(*dims):
@@ -473,25 +485,27 @@
     )(se, se, mr, mr, g, sw, mw, sf)
 
 
-def ctx_sums(short_rows, medium_part):
+def ctx_shares(short_rows, medium_part):
     count = lax.axis_size("ctx")
-    channels = short_rows.shape[1]
-    medium_length = medium_part.shape[0]
-    depth = medium_length // count
-    width = short_rows.size // (count * depth)
+    depth = medium_part.shape[0] // count
     terms = jnp.concatenate(
         [
-            medium_part.reshape(count, depth, channels),
-            short_rows.astype(BF16).reshape(count, depth, width),
+            medium_part.reshape(count, depth, -1),
+            short_rows.reshape(count, depth, -1),
         ],
         axis=2,
     )
-    shares = lax.all_to_all(terms, "ctx", 0, 0, tiled=True)
+    return lax.all_to_all(terms, "ctx", 0, 0, tiled=True)
+
+
+def ctx_totals(shares):
+    count, depth, width = shares.shape
+    channels = width * count * depth // (count * depth + 8)
     total = jnp.sum(shares.astype(F32), axis=0).astype(BF16)
-    copies = jnp.broadcast_to(total[None], (count,) + total.shape)
+    copies = jnp.broadcast_to(total[None], shares.shape)
     totals = lax.all_to_all(copies, "ctx", 0, 0, tiled=True).astype(F32)
-    medium_total = totals[:, :, :channels].reshape(medium_length, channels)
-    short_total = totals[:, :, channels:].reshape(short_rows.shape)[:7]
+    medium_total = totals[:, :, :channels].reshape(count * depth, channels)
+    short_total = totals[:, :, channels:].reshape(8, channels)[:7]
     return short_total, medium_total
 
 
@@ -509,14 +523,18 @@
 
     last, first = edges(se, mr, g, sw, mw, sf)
     before = lax.ppermute(last, "ctx", onward)
+    before, first = lax.optimization_barrier((before, first))
     ahead = lax.ppermute(first, "ctx", backward)
-    feats, ps, product, own_d = blocks_call(
+    q1, z1, k2, v2, ps, product, own_d = blocks_call(
         "forward",
         forward_kernel,
         [se, mr, g, before, sw, mw, sf],
         [fwd],
         [
-            ((4, rows), F32),
+            ((rows,), F32),
+            ((rows,), F32),
+            ((rows,), F32),
+            ((rows,), F32),
             ((rows,), BF16),
             ((rows,), BF16),
             ((POINTS,), F32),
@@ -531,17 +549,18 @@
         4000,
     )
     behind = lax.ppermute(product[rows - 128 :], "ctx", onward)
-    medium_part, short_rows, w2, dy1, feats_ahead, product_ahead = blocks_call(
+    medium_part, short_rows, w2, dy1, feats_ahead, v2_ahead, product_ahead = blocks_call(
         "middle",
         functools.partial(middle_kernel, norm_factor),
-        [feats, ps, product, own_d, mf, rate, before, last, ahead, sw, mw, sf],
+        [q1, k2, ps, product, own_d, mf, rate, before, last, ahead, sw, mw, sf],
         [fwd, inv],
         [
             ((128,), BF16),
-            ((8,), F32),
+            ((8,), BF16),
             ((end,), F32),
             ((end,), F32),
-            ((6, REACH), F32),
+            ((5, REACH), F32),
+            ((REACH,), F32),
             ((REACH,), BF16),
         ],
         [
@@ -556,41 +575,37 @@
         4000,
     )
     medium_part, behind = lax.optimization_barrier((medium_part, behind))
-    se_out, mr_out = blocks_call(
-        "backward",
-        backward_kernel,
-        [
-            feats,
-            feats_ahead,
-            w2,
-            dy1,
-            product,
-            mf,
-            rate,
-            behind,
-            product_ahead,
-            se,
-            before,
-            g,
-            ahead,
-            sw,
-            mw,
-            sf,
-        ],
-        [fwd, rim, inv],
-        [((3, rows), BF16), ((2, rows), BF16)],
+    shares = ctx_shares(short_rows, medium_part)
+    (se_out,) = blocks_call(
+        "se_backward",
+        se_backward_kernel,
+        [q1, z1, feats_ahead, dy1, se, before, sw, sf],
+        [],
+        [((3, rows), BF16)],
         [
             f32_rows(2, PAD + rows),
+            f32_rows(32),
+            f32_rows(3, end + 16),
+            f32_rows(end + 16),
+        ],
+        2000,
+    )
+    shares, se_out, v2 = lax.optimization_barrier((shares, se_out, v2))
+    short_total, medium_total = ctx_totals(shares)
+    (mr_out,) = blocks_call(
+        "mr_backward",
+        mr_backward_kernel,
+        [v2, v2_ahead, w2, product, mf, rate, behind, product_ahead, g, ahead, mw],
+        [fwd, rim, inv],
+        [((2, rows), BF16)],
+        [
             bf16_rows(256),
             pltpu.VMEM((end, BLOCK), F32),
             f32_rows(32),
             f32_rows(2, end + 16),
-            f32_rows(3, end + 16),
-            f32_rows(end + 16),
-        ],
-        4000,
-    )
-    short_total, medium_total = ctx_sums(short_rows, medium_part)
+        ],
+        2000,
+    )
     return (
         jnp.transpose(se_out, (1, 0, 2)),
         jnp.transpose(mr_out, (1, 0, 2)),

time: 93.5 us -> 86 us (0.920)
  blocking collectives: 24.5 us -> 0 us
  starting transfers between devices: 16 us -> 29.5 us
  Pallas kernels: 29.9 us -> 31.9 us
  waiting for transfers between devices: 7.62 us -> 9.02 us
    all_to_all x1 -> x0, blocking collectives: 24.5 us -> none  [ctx_sums(): shares = lax.all_to_all(terms, 'ctx', 0, 0, tiled=True)]
    all_to_all x1 -> x2, starting transfers between devices: 5.86 us -> 20.2 us  [the longest x1 15.1 us: ctx_shares(): return lax.all_to_all(terms, 'ctx', 0, 0, tiled=True)]
    all_to_all x1 -> x2, waiting for transfers between devices: 0.01 us -> 6.81 us  [the longest x1 6.81 us: ctx_shares(): return lax.all_to_all(terms, 'ctx', 0, 0, tiled=True)]
    ppermute x1, waiting for transfers between devices: 7.61 us -> 2.2 us  [local(): before = lax.ppermute(last, 'ctx', onward)]
    pallas_call x3 -> x4, Pallas kernels: 27.6 us -> 29.6 us  [blocks_call(): pl.pallas_call(body, grid=(channels // BLOCK,), in_specs=[rows_of(*a.shap...]
    ppermute x1, starting transfers between devices: 4.55 us -> 3.18 us  [local(): before = lax.ppermute(last, 'ctx', onward)]
  transfers between devices with their start and end apart: 4 -> 5, of which waited for: 1 -> 2; matrix products, arithmetic and copies ran while one was open for 5% -> 6% of each run, Pallas kernels for 30% -> 35%
where the time goes in v1:
time: 86 us; the launch traced here: 84.8 us
  Pallas kernels  31.9 us (37%)
  starting transfers between devices  29.5 us (34%)
  local copies, waits for them, and re-layouts  12.4 us (14%)
  waiting for transfers between devices  9.02 us (10%)
  other arithmetic  1.26 us (1%)
    pallas_call x4, Pallas kernels, blocks_call(): pl.pallas_call(body, grid=(channels // BLOCK,), in_specs=[rows_of(*a.shap...  29.6 us
    all_to_all x1, starting transfers between devices, ctx_shares(): return lax.all_to_all(terms, 'ctx', 0, 0, tiled=True)  15.1 us
    all_to_all x1, waiting for transfers between devices, ctx_shares(): return lax.all_to_all(terms, 'ctx', 0, 0, tiled=True)  6.81 us
    unnamed x8, local copies, waits for them, and re-layouts  6.48 us
    all_to_all x1, starting transfers between devices, ctx_totals(): totals = lax.all_to_all(copies, 'ctx', 0, 0, tiled=True).astype(F32)  5.19 us
    ppermute x1, starting transfers between devices, local(): behind = lax.ppermute(product[rows - 128:], 'ctx', onward)  4.8 us
    ppermute x1, starting transfers between devices, local(): before = lax.ppermute(last, 'ctx', onward)  3.18 us
    pallas_call x1, Pallas kernels, edges(): pl.pallas_call(edge_kernel, grid=(channels // wide,), in_specs=[part((3,)...  2.31 us
  transfers between devices with their start and end apart: 5, of which 2 were waited for; matrix products, arithmetic and copies ran while one was open for 6% of the time, Pallas kernels for 35%

profile of v1, /device:TPU:16, one launch (start us, length us, event | category | flops | bytes accessed | tf_op | source)
XLA Modules:
  0.0 84.8 jit_solution(18153379139844076317)
XLA Ops:
  0.6 2.5 %copy.18 = bf16[256,2,1024]{2,0,1:T(8,128)(2,1)} copy(bf16[256,2,1024]{2,1,0:T(2,128)(2,1)} %param.12) | data formatting | bytes 2097152 | tf_op args[1]
  3.1 2.3 %edges.1 = (bf16[32,1024]{1,0:T(8,128)(2,1)}, bf16[176,1024]{1,0:T(8,128)(2,1)}) custom-call(bf16[3,256,1024]{2,1,0:T(8,128)(2,1)} %bitcast.7, bf16[3,256,1024]{2,1,0:T(8,128)(2,1)} %bitcast.8, bf16[2,256,1024]{2,1,0:T(8,128)(2,1)} %bitcast.11, bf16[2,256,1024]{2,1,0:T(8,128)(2,1)} %bitcast.12, bf16[256,1024]{1,0:T(8,128)(2,1)} %g_ref.5, ...), custom_call_target="tpu_custom_call" | custom-call | tf_op jit(solution)/shard_map/edges/pallas_call | solution.py:458
  5.4 3.2 %collective-permute-start = (bf16[32,1024]{1,0:T(8,128)(2,1)}, bf16[32,1024]{1,0:T(8,128)(2,1)S(1)}, u32[]{:S(2)}, u32[]{:S(2)}) collective-permute-start(bf16[32,1024]{1,0:T(8,128)(2,1)} %get-tuple-element.27.last_ref), channel_id=1, source_target_pairs={{0,4},{4,8},{8,12},{12,16},{16,20},{20,24},{24,28},{28,32},{32,36}... | collective-permute-start | bytes 196616 | tf_op jit(solution)/shard_map/ppermute | solution.py:525
  8.6 2.2 %collective-permute-done.before_ref = bf16[32,1024]{1,0:T(8,128)(2,1)S(1)} collective-permute-done((bf16[32,1024]{1,0:T(8,128)(2,1)}, bf16[32,1024]{1,0:T(8,128)(2,1)S(1)}, u32[]{:S(2)}, u32[]{:S(2)}) %collective-permute-start) | collective-permute-done | bytes 65568 | tf_op jit(solution)/shard_map/ppermute | solution.py:525
  10.8 0.0 copy-start.1
  10.8 1.3 %collective-permute-start.1 = (bf16[176,1024]{1,0:T(8,128)(2,1)}, bf16[176,1024]{1,0:T(8,128)(2,1)S(1)}, u32[]{:S(2)}, u32[]{:S(2)}) collective-permute-start(bf16[176,1024]{1,0:T(8,128)(2,1)} %get-tuple-element.35), channel_id=1, source_target_pairs={{4,0},{8,4},{12,8},{16,12},{20,16},{24,20},{28,24},{32,28},{36,32}... | collective-permute-start | bytes 1081352 | tf_op jit(solution)/shard_map/ppermute | solution.py:527
  12.1 0.0 copy-done.1
  12.1 6.9 %forward.1 = (f32[256,1024]{1,0:T(8,128)}, f32[256,1024]{1,0:T(8,128)}, f32[256,1024]{1,0:T(8,128)}, f32[256,1024]{1,0:T(8,128)}, bf16[256,1024]{1,0:T(8,128)(2,...) custom-call(bf16[3,256,1024]{2,1,0:T(8,128)(2,1)} %bitcast.9, bf16[2,256,1024]{2,1,0:T(8,128)(2,1)} %bitcast.13, ...), custom_call_target="tpu_custom_call" | custom-call | flops 1048576000 | bytes 4194304 | tf_op jit(solution)/shard_map/forward/pallas_call | solution.py:435
  19.0 1.0 %slice.14 = bf16[128,1024]{1,0:T(8,128)(2,1)S(1)} slice(bf16[256,1024]{1,0:T(8,128)(2,1)} %get-tuple-element.33.pb.own_ref), slice={[128:256], [0:1024]} | slice | bytes 524288 | tf_op jit(solution)/shard_map/slice | solution.py:551
  20.0 4.8 %collective-permute-start.2 = (bf16[128,1024]{1,0:T(8,128)(2,1)S(1)}, bf16[128,1024]{1,0:T(8,128)(2,1)S(1)}, u32[]{:S(2)}, u32[]{:S(2)}) collective-permute-start(bf16[128,1024]{1,0:T(8,128)(2,1)S(1)} %slice.14), channel_id=1, source_target_pairs={{0,4},{4,8},{8,12},{12,16},{16,20},{20,24},{24,28},{28,32},{32,36}... | collective-permute-start | bytes 786440 | tf_op jit(solution)/shard_map/ppermute | solution.py:551
  24.8 0.0 collective-permute-done.1.ahead_ref
  24.8 0.0 copy-start
  24.8 0.7 copy-done
  25.5 9.0 %middle.1 = (bf16[128,1024]{1,0:T(8,128)(2,1)}, bf16[8,1024]{1,0:T(8,128)(2,1)}, f32[272,1024]{1,0:T(8,128)}, f32[272,1024]{1,0:T(8,128)}, f32[5,16,1024]{2,1,0:...) custom-call(f32[256,1024]{1,0:T(8,128)} %get-tuple-element.30.q1_ref, f32[256,1024]{1,0:T(8,128)} %get-tuple-element.31.k2_ref, ...), custom_call_target="tpu_custom_call" | custom-call | flops 1048576000 | bytes 4194304 | tf_op jit(solution)/shard_map/middle/pallas_call | solution.py:435
  34.6 0.8 reshape.21
  35.4 0.0 collective-permute-done.2.behind_ref
  35.4 0.0 copy-start.2
  35.4 1.1 %reshape.20 = bf16[64,2,1024]{2,1,0:T(2,128)(2,1)S(1)} reshape(bf16[128,1024]{1,0:T(8,128)(2,1)} %get-tuple-element.37) | data formatting | bytes 524288 | tf_op jit(solution)/shard_map/reshape | solution.py:493
  36.6 1.0 %pad_maximum_fusion = bf16[64,2,1088]{2,1,0:T(2,128)(2,1)} fusion(bf16[64,2,64]{2,1,0:T(2,128)(2,1)S(1)} %reshape.21, bf16[64,2,1024]{2,1,0:T(2,128)(2,1)S(1)} %reshape.20), kind=kLoop, calls=%fused_computation.1 | loop fusion | flops 557056 | bytes 557056 | tf_op jit(solution)/shard_map/concatenate | solution.py:491
  37.6 15.1 %all-to-all-start = ((bf16[64,2,1088]{2,1,0:T(2,128)(2,1)}), bf16[64,2,1088]{2,1,0:T(2,128)(2,1)S(1)}, u32[]{:S(2)}, u32[]{:S(2)}) async-start(bf16[64,2,1088]{2,1,0:T(2,128)(2,1)} %pad_maximum_fusion), calls=%async_computation | async-start | bytes 589824 | tf_op jit(solution)/shard_map/all_to_all | solution.py:498
  52.6 5.1 %se_backward.1 = bf16[3,256,1024]{2,1,0:T(8,128)(2,1)} custom-call(f32[256,1024]{1,0:T(8,128)} %get-tuple-element.30.q1_ref, f32[256,1024]{1,0:T(8,128)} %get-tuple-element.39.z1_ref, f32[5,16,1024]{2,1,0:T(8,128)} %get-tuple-element.40.feats_ahead, f32[272,1024]{1,0:T(8,128)} %get-tuple-element.41.dy1, bf16[3,256,1024]{2,1,0:T(8,128)(2,1)} %bitcast.10, ...), custom_call_target="tpu_custom_call" | custom-call | flops 524288000 | bytes 4194304 | tf_op jit(solution)/shard_map/se_backward/pallas_call | solution.py:435
  57.7 0.0 copy-done.2
  57.7 6.8 %all-to-all-done = bf16[64,2,1088]{2,1,0:T(2,128)(2,1)S(1)} async-done(((bf16[64,2,1088]{2,1,0:T(2,128)(2,1)}), bf16[64,2,1088]{2,1,0:T(2,128)(2,1)S(1)}, u32[]{:S(2)}, u32[]{:S(2)}) %all-to-all-start) | async-done | bytes 278560 | tf_op jit(solution)/shard_map/all_to_all | solution.py:498
  64.6 0.3 reduce_sum.12
  64.8 0.9 %broadcast_in_dim.10 = bf16[64,2,1088]{2,1,0:T(2,128)(2,1)} broadcast(bf16[2,1088]{1,0:T(2,128)(2,1)S(1)} %reduce_sum.12), dimensions={1,2} | broadcast | bytes 282880 | tf_op jit(solution)/shard_map/broadcast_in_dim | solution.py:505
  65.7 5.2 %all-to-all-start.1 = ((bf16[64,2,1088]{2,1,0:T(2,128)(2,1)}), bf16[64,2,1088]{2,1,0:T(2,128)(2,1)S(1)}, u32[]{:S(2)}, u32[]{:S(2)}) async-start(bf16[64,2,1088]{2,1,0:T(2,128)(2,1)} %broadcast_in_dim.10), calls=%async_computation.1 | async-start | bytes 589824 | tf_op jit(solution)/shard_map/all_to_all | solution.py:506
  70.9 8.6 %mr_backward.1 = bf16[2,256,1024]{2,1,0:T(8,128)(2,1)} custom-call(f32[256,1024]{1,0:T(8,128)} %get-tuple-element.44.v2, f32[16,1024]{1,0:T(8,128)} %get-tuple-element.45.v2_ahead, f32[272,1024]{1,0:T(8,128)} %get-tuple-element.46.w2, bf16[256,1024]{1,0:T(8,128)(2,1)} %get-tuple-element.33.pb.own_ref, f32[128,1024]{1,0:T(8,128)} %mf_ref.3, ...), custom_call_target="tpu_custom_call" | custom-call | flops 524288000 | bytes 4194304 | tf_op jit(solution)/shard_map/mr_backward/pallas_call | solution.py:435
  79.5 3.3 %copy.16 = bf16[256,2,1024]{2,1,0:T(2,128)(2,1)} copy(bf16[256,2,1024]{2,0,1:T(8,128)(2,1)} %bitcast.14) | data formatting | bytes 2097152
  82.7 0.0 all-to-all-done.1
  82.8 0.7 slice.16
  83.5 0.2 slice.19
  83.7 1.2 %reshape.22 = f32[128,1024]{1,0:T(8,128)} reshape(f32[64,2,1024]{2,1,0:T(2,128)S(1)} %slice.19) | data formatting | bytes 1048576 | tf_op jit(solution)/shard_map/reshape | solution.py:507
  (1 shorter events, 0.0 us)
Async XLA Ops:
  5.4 5.4 %collective-permute-start = (bf16[32,1024]{1,0:T(8,128)(2,1)}, bf16[32,1024]{1,0:T(8,128)(2,1)S(1)}, u32[]{:S(2)}, u32[]{:S(2)}) collective-permute-start(bf16[32,1024]{1,0:T(8,128)(2,1)} %get-tuple-element.27.last_ref), channel_id=1, source_target_pairs={{0,4},{4,8},{8,12},{12,16},{16,20},{20,24},{24,28},{28,32},{32,36}... | collective-permute-start | bytes 196616 | tf_op jit(solution)/shard_map/ppermute | solution.py:525
  10.8 1.3 %copy-start.1 = (bf16[32,1024]{1,0:T(8,128)(2,1)}, bf16[32,1024]{1,0:T(8,128)(2,1)S(1)}, u32[]{:S(2)}) copy-start(bf16[32,1024]{1,0:T(8,128)(2,1)S(1)} %collective-permute-done.before_ref) | copy-start | bytes 196612
  10.8 14.0 %collective-permute-start.1 = (bf16[176,1024]{1,0:T(8,128)(2,1)}, bf16[176,1024]{1,0:T(8,128)(2,1)S(1)}, u32[]{:S(2)}, u32[]{:S(2)}) collective-permute-start(bf16[176,1024]{1,0:T(8,128)(2,1)} %get-tuple-element.35), channel_id=1, source_target_pairs={{4,0},{8,4},{12,8},{16,12},{20,16},{24,20},{28,24},{32,28},{36,32}... | collective-permute-start | bytes 1081352 | tf_op jit(solution)/shard_map/ppermute | solution.py:527
  20.0 15.4 %collective-permute-start.2 = (bf16[128,1024]{1,0:T(8,128)(2,1)S(1)}, bf16[128,1024]{1,0:T(8,128)(2,1)S(1)}, u32[]{:S(2)}, u32[]{:S(2)}) collective-permute-start(bf16[128,1024]{1,0:T(8,128)(2,1)S(1)} %slice.14), channel_id=1, source_target_pairs={{0,4},{4,8},{8,12},{12,16},{16,20},{20,24},{24,28},{28,32},{32,36}... | collective-permute-start | bytes 786440 | tf_op jit(solution)/shard_map/ppermute | solution.py:551
  24.8 0.7 copy-start
  35.4 22.3 %copy-start.2 = (bf16[128,1024]{1,0:T(8,128)(2,1)}, bf16[128,1024]{1,0:T(8,128)(2,1)S(1)}, u32[]{:S(2)}) copy-start(bf16[128,1024]{1,0:T(8,128)(2,1)S(1)} %collective-permute-done.2.behind_ref) | copy-start | bytes 786436
  37.6 27.0 %all-to-all-start = ((bf16[64,2,1088]{2,1,0:T(2,128)(2,1)}), bf16[64,2,1088]{2,1,0:T(2,128)(2,1)S(1)}, u32[]{:S(2)}, u32[]{:S(2)}) async-start(bf16[64,2,1088]{2,1,0:T(2,128)(2,1)} %pad_maximum_fusion), calls=%async_computation | async-start | bytes 589824 | tf_op jit(solution)/shard_map/all_to_all | solution.py:498
  65.7 17.0 %all-to-all-start.1 = ((bf16[64,2,1088]{2,1,0:T(2,128)(2,1)}), bf16[64,2,1088]{2,1,0:T(2,128)(2,1)S(1)}, u32[]{:S(2)}, u32[]{:S(2)}) async-start(bf16[64,2,1088]{2,1,0:T(2,128)(2,1)} %broadcast_in_dim.10), calls=%async_computation.1 | async-start | bytes 589824 | tf_op jit(solution)/shard_map/all_to_all | solution.py:506

commit v2 on v1

--- a/solution.py
+++ b/solution.py
@@ -15,6 +15,7 @@
 LANES = 128
 BLOCK = 256
 PAD = 16
+LIMIT = 56 * 2**20
 REACH = 16
 POINTS = 400
 HALF = POINTS // 2
@@ -94,39 +95,15 @@
     return jnp.concatenate([fr * sr - fi * si, fr * si + fi * sr, zeros], axis=0)
 
 
-def edge_kernel(
-    se_start, se_end, mr_start, mr_end, g_ref, sw_ref, mw_ref, sf_ref, last_ref, first_ref, x, q1, ps, y1, tail
-):
-    for h in range(g_ref.shape[1] // LANES):
+def last_kernel(se_end, mr_end, sw_ref, sf_ref, last_ref, x, q1, ps, y1, tail):
+    for h in range(se_end.shape[2] // LANES):
         lanes = lanes_of(h)
         sw = feature_taps(sw_ref, lanes)
-        mw = feature_taps(mw_ref, lanes)
         sf = short_taps(sf_ref, lanes)
-        x[3, 0:PAD, :] = jnp.zeros((PAD, LANES), F32)
-        for a, n in chunks(0, 144):
-            x[3, pl.ds(PAD + a, n), :] = mr_start[0, pl.ds(a, n), lanes].astype(F32)
-        for a, n in chunks(0, 144):
-            q2 = weighted(x, (3,), PAD + a, n, mw[0], -1)
-            first_ref[pl.ds(a, n), lanes] = (
-                g_ref[pl.ds(a, n), lanes].astype(F32) * q2
-            ).astype(BF16)
-        for p in range(3):
-            x[p, 0:16, :] = se_start[p, :, lanes].astype(F32)
-        x[4, 0:16, :] = mr_start[1, 0:16, lanes].astype(F32)
-        y1[0:16, :] = g_ref[0:16, lanes].astype(F32)
-        tail[...] = jnp.zeros((32, LANES), F32)
-        tail[0:2, :] = y1[0:2, :]
-        tail[2:4, :] = x[3, PAD : PAD + 2, :]
-        tail[4:14, :] = x[4, 0:10, :]
-        tail[14:22, :] = x[0, 0:8, :]
-        tail[22:24, :] = x[1, 0:2, :]
-        tail[24:26, :] = x[2, 0:2, :]
-        first_ref[144:176, lanes] = tail[...].astype(BF16)
-
         for p in range(3):
             x[p, 0:32, :] = se_end[p, :, lanes].astype(F32)
         for p in range(2):
-            x[3 + p, 0:32, :] = mr_end[p, :, lanes].astype(F32)
+            x[3 + p, 0:32, :] = mr_end[:, p, lanes].astype(F32)
         k1 = weighted(x, (1,), 8, 24, sw[1], -1)
         v1 = weighted(x, (2,), 8, 24, sw[2], -1)
         ps[8:32, :] = rounded(k1 * v1)
@@ -138,6 +115,32 @@
         for p in range(5):
             tail[8 + 2 * p : 10 + 2 * p, :] = x[p, 30:32, :]
         last_ref[:, lanes] = tail[...].astype(BF16)
+
+
+def first_kernel(se_start, mr_start, g_ref, mw_ref, after_ref, first_ref, x, y1, tail):
+    for h in range(g_ref.shape[1] // LANES):
+        lanes = lanes_of(h)
+        mw = feature_taps(mw_ref, lanes)
+        x[3, 0:PAD, :] = jnp.zeros((PAD, LANES), F32)
+        for a, n in chunks(0, 144):
+            x[3, pl.ds(PAD + a, n), :] = mr_start[pl.ds(a, n), 0, lanes].astype(F32)
+        for a, n in chunks(0, 144):
+            q2 = weighted(x, (3,), PAD + a, n, mw[0], -1)
+            first_ref[pl.ds(a, n), lanes] = (
+                g_ref[pl.ds(a, n), lanes].astype(F32) * q2
+            ).astype(BF16)
+        for p in range(3):
+            x[p, 0:16, :] = se_start[p, :, lanes].astype(F32)
+        x[4, 0:16, :] = mr_start[0:16, 1, lanes].astype(F32)
+        y1[0:16, :] = g_ref[0:16, lanes].astype(F32)
+        tail[...] = jnp.zeros((32, LANES), F32)
+        tail[0:2, :] = y1[0:2, :]
+        tail[2:4, :] = x[3, PAD : PAD + 2, :]
+        tail[4:14, :] = x[4, 0:10, :]
+        tail[14:22, :] = x[0, 0:8, :]
+        tail[22:24, :] = x[1, 0:2, :]
+        tail[24:26, :] = x[2, 0:2, :]
+        first_ref[144:176, lanes] = tail[...].astype(BF16)
 
 
 def medium_spectrum(mf_ref, rate_ref, fwd_ref):
@@ -161,6 +164,7 @@
     v2_ref,
     ps_ref,
     pb,
+    edge_ref,
     own_d,
     x,
     ps,
@@ -183,7 +187,7 @@
             for p in range(3):
                 x[p, pl.ds(PAD + t, n), :] = se_ref[p, pl.ds(t, n), lanes].astype(F32)
             for p in range(2):
-                x[3 + p, pl.ds(PAD + t, n), :] = mr_ref[p, pl.ds(t, n), lanes].astype(F32)
+                x[3 + p, pl.ds(PAD + t, n), :] = mr_ref[pl.ds(t, n), p, lanes].astype(F32)
         for t, n in chunks(0, rows):
             r, at = PAD + t, pl.ds(t, n)
             key = weighted(x, (1,), r, n, sw[1], -1)
@@ -200,7 +204,10 @@
             value = weighted(y1, (), r, n, mw[2], -1)
             k2_ref[at, lanes] = key
             v2_ref[at, lanes] = value
-            pb[at, lanes] = (key * value).astype(BF16)
+            product = (key * value).astype(BF16)
+            pb[at, lanes] = product
+            if t >= rows - 128:
+                edge_ref[pl.ds(t - (rows - 128), n), lanes] = product
             query = weighted(x, (3,), r, n, mw[0], -1)
             high, low = split(g_ref[at, lanes].astype(F32) * query)
             db[0, at, lanes] = high
@@ -230,13 +237,12 @@
     sf_ref,
     fwd_ref,
     inv_ref,
-    medium_out,
-    short_out,
     w2_out,
     dy1_out,
     feats_out,
     v2_out,
     product_out,
+    terms,
     x,
     ps,
     y1,
@@ -294,7 +300,10 @@
     spread = wide_dot(inv_ref, slice(None), slice(None), product_of(kernel, dd, True))
     w2_out[...] = spread
     lagged = wide_dot(inv_ref, slice(0, 128), slice(None), product_of(pp, dd, True))
-    medium_out[...] = (lagged * (damping * norm_factor)).astype(BF16)
+    step = pl.program_id(0)
+    lagged = (lagged * (damping * norm_factor)).astype(BF16)
+    columns = pl.ds(pl.multiple_of(step * BLOCK, BLOCK), BLOCK)
+    terms[:, :, columns] = lagged.reshape(terms.shape[0], terms.shape[1], BLOCK)
 
     for h in range(BLOCK // LANES):
         lanes = lanes_of(h)
@@ -321,7 +330,10 @@
         for j in range(7):
             tail[j : j + 1, :] = jnp.sum(sums[j], axis=0, keepdims=True)
         tail[7:8, :] = jnp.zeros((1, LANES), F32)
-        short_out[:, lanes] = (tail[0:16, :] * norm_factor).astype(BF16)[0:8]
+        sums = tail[0:8, :] * norm_factor
+        sums = jnp.concatenate([sums[:, None, :], jnp.zeros((8, 1, LANES), F32)], axis=1)
+        group = pl.ds(pl.multiple_of((step * (BLOCK // LANES) + h) * 8, 8), 8)
+        terms[group, :, terms.shape[2] - LANES :] = sums.astype(BF16)
 
 
 def spans(rows):
@@ -410,8 +422,8 @@
             upstream = tail[0:REACH, :] if base else g_ref[at, lanes].astype(F32)
             d[0, at, :] = upstream * z2[at, lanes]
         for t, n in chunks(0, rows):
-            for p in range(2):
-                mr_out[p, pl.ds(t, n), lanes] = weighted(d, (p,), t, n, mw[p], 1).astype(BF16)
+            pair = [weighted(d, (p,), t, n, mw[p], 1)[:, None, :] for p in range(2)]
+            mr_out[pl.ds(t, n), :, lanes] = jnp.concatenate(pair, axis=1).astype(BF16)
 
 
 def rows_of(*dims):
@@ -419,7 +431,7 @@
 
 
 def fixed(array):
-    return pl.BlockSpec(array.shape, lambda i: (0,) * array.ndim)
+    return pl.BlockSpec(array.shape, lambda i: (0,) * len(array.shape))
 
 
 def f32_rows(*dims):
@@ -430,16 +442,17 @@
     return pltpu.VMEM(dims + (BLOCK,), BF16)
 
 
-def blocks_call(name, body, arrays, tables, outs, scratch, flops):
+def blocks_call(name, body, arrays, tables, outs, scratch, flops, whole=()):
     channels = arrays[0].shape[-1]
     return pl.pallas_call(
         body,
         grid=(channels // BLOCK,),
         in_specs=[rows_of(*a.shape[:-1]) for a in arrays] + [fixed(t) for t in tables],
-        out_specs=[rows_of(*dims) for dims, _ in outs],
-        out_shape=[jax.ShapeDtypeStruct(dims + (channels,), kind) for dims, kind in outs],
+        out_specs=[rows_of(*dims) for dims, _ in outs] + [fixed(a) for a in whole],
+        out_shape=[jax.ShapeDtypeStruct(dims + (channels,), kind) for dims, kind in outs]
+        + list(whole),
         scratch_shapes=scratch,
-        compiler_params=pltpu.CompilerParams(vmem_limit_bytes=56 * 2**20),
+        compiler_params=pltpu.CompilerParams(vmem_limit_bytes=LIMIT),
         cost_estimate=pl.CostEstimate(
             flops=flops * 256 * channels, bytes_accessed=16 * 256 * channels, transcendentals=0
         ),
@@ -447,65 +460,60 @@
     )(*arrays, *tables)
 
 
-def edges(se, mr, g, sw, mw, sf):
-    rows, channels = g.shape
+def edge_call(name, body, parts, out_rows, scratch):
+    channels = parts[0][0].shape[-1]
     wide = min(channels, 512)
 
     def part(lead, count, at):
         zeros = (0,) * len(lead)
         return pl.BlockSpec(lead + (count, wide), lambda i: zeros + (at, i))
 
+    def pairs(count, at):
+        return pl.BlockSpec((count, 2, wide), lambda i: (at, 0, i))
+
     return pl.pallas_call(
-        edge_kernel,
+        body,
         grid=(channels // wide,),
         in_specs=[
-            part((3,), 16, 0),
-            part((3,), 32, rows // 32 - 1),
-            part((2,), 144, 0),
-            part((2,), 32, rows // 32 - 1),
-            part((), 144, 0),
-            part((3,), 3, 0),
-            part((3,), 3, 0),
-            part((), 7, 0),
+            pairs(count, at) if a.ndim == 3 and a.shape[1] == 2 else part(a.shape[:-2], count, at)
+            for a, count, at in parts
         ],
-        out_specs=[part((), 32, 0), part((), 176, 0)],
-        out_shape=[
-            jax.ShapeDtypeStruct((32, channels), BF16),
-            jax.ShapeDtypeStruct((176, channels), BF16),
-        ],
-        scratch_shapes=[
-            f32_rows(5, 160),
-            f32_rows(32),
-            f32_rows(32),
-            f32_rows(32),
-            f32_rows(32),
-        ],
-        compiler_params=pltpu.CompilerParams(vmem_limit_bytes=56 * 2**20),
-        name="edges",
-    )(se, se, mr, mr, g, sw, mw, sf)
-
-
-def ctx_shares(short_rows, medium_part):
-    count = lax.axis_size("ctx")
-    depth = medium_part.shape[0] // count
-    terms = jnp.concatenate(
-        [
-            medium_part.reshape(count, depth, -1),
-            short_rows.reshape(count, depth, -1),
-        ],
-        axis=2,
-    )
-    return lax.all_to_all(terms, "ctx", 0, 0, tiled=True)
+        out_specs=part((), out_rows, 0),
+        out_shape=jax.ShapeDtypeStruct((out_rows, channels), BF16),
+        scratch_shapes=scratch,
+        compiler_params=pltpu.CompilerParams(vmem_limit_bytes=LIMIT),
+        name=name,
+    )(*(a for a, _, _ in parts))
+
+
+def edges(se, mr, g, sw, mw, sf):
+    end = g.shape[0] // 32 - 1
+    last = edge_call(
+        "last_rows",
+        last_kernel,
+        [(se, 32, end), (mr, 32, end), (sw, 3, 0), (sf, 7, 0)],
+        32,
+        [f32_rows(5, 32)] + [f32_rows(32)] * 4,
+    )
+    first = edge_call(
+        "first_rows",
+        first_kernel,
+        [(se, 16, 0), (mr, 144, 0), (g, 144, 0), (mw, 3, 0), (last, 32, 0)],
+        176,
+        [f32_rows(5, 160), f32_rows(32), f32_rows(32)],
+    )
+    return last, first
 
 
 def ctx_totals(shares):
     count, depth, width = shares.shape
-    channels = width * count * depth // (count * depth + 8)
+    channels = width - LANES
     total = jnp.sum(shares.astype(F32), axis=0).astype(BF16)
     copies = jnp.broadcast_to(total[None], shares.shape)
-    totals = lax.all_to_all(copies, "ctx", 0, 0, tiled=True).astype(F32)
+    totals = lax.all_to_all(copies, "ctx", 0, 0, tiled=True).reshape(64, 2, width).astype(F32)
     medium_total = totals[:, :, :channels].reshape(count * depth, channels)
-    short_total = totals[:, :, channels:].reshape(8, channels)[:7]
+    short_total = totals[: channels // 16, 0, channels:].reshape(-1, 8, LANES)
+    short_total = jnp.swapaxes(short_total, 0, 1).reshape(8, channels)[:7]
     return short_total, medium_total
 
 
@@ -516,7 +524,7 @@
     norm_factor = 1.0 / math.sqrt(rows * count)
     fwd, rim, inv = (jnp.asarray(table) for table in tables)
     se = jnp.transpose(se_input, (1, 0, 2))
-    mr = jnp.transpose(mr_input, (1, 0, 2))
+    mr = mr_input
     onward = [(i, i + 1) for i in range(count - 1)]
     backward = [(i, i - 1) for i in range(1, count)]
     rate = decay_rate[None, :]
@@ -525,7 +533,7 @@
     before = lax.ppermute(last, "ctx", onward)
     before, first = lax.optimization_barrier((before, first))
     ahead = lax.ppermute(first, "ctx", backward)
-    q1, z1, k2, v2, ps, product, own_d = blocks_call(
+    q1, z1, k2, v2, ps, product, edge, own_d = blocks_call(
         "forward",
         forward_kernel,
         [se, mr, g, before, sw, mw, sf],
@@ -537,6 +545,7 @@
             ((rows,), F32),
             ((rows,), BF16),
             ((rows,), BF16),
+            ((128,), BF16),
             ((POINTS,), F32),
         ],
         [
@@ -548,15 +557,12 @@
         ],
         4000,
     )
-    behind = lax.ppermute(product[rows - 128 :], "ctx", onward)
-    medium_part, short_rows, w2, dy1, feats_ahead, v2_ahead, product_ahead = blocks_call(
+    w2, dy1, feats_ahead, v2_ahead, product_ahead, terms = blocks_call(
         "middle",
         functools.partial(middle_kernel, norm_factor),
         [q1, k2, ps, product, own_d, mf, rate, before, last, ahead, sw, mw, sf],
         [fwd, inv],
         [
-            ((128,), BF16),
-            ((8,), BF16),
             ((end,), F32),
             ((end,), F32),
             ((5, REACH), F32),
@@ -573,9 +579,12 @@
             f32_rows(end + 16),
         ],
         4000,
-    )
-    medium_part, behind = lax.optimization_barrier((medium_part, behind))
-    shares = ctx_shares(short_rows, medium_part)
+        [jax.ShapeDtypeStruct((64, 2, channels + LANES), BF16)],
+    )
+    terms, edge = lax.optimization_barrier((terms, edge))
+    behind = lax.ppermute(edge, "ctx", onward)
+    terms = terms.reshape(count, 128 // count, channels + LANES)
+    shares = lax.all_to_all(terms, "ctx", 0, 0, tiled=True)
     (se_out,) = blocks_call(
         "se_backward",
         se_backward_kernel,
@@ -590,14 +599,14 @@
         ],
         2000,
     )
-    shares, se_out, v2 = lax.optimization_barrier((shares, se_out, v2))
+    shares, se_out, behind = lax.optimization_barrier((shares, se_out, behind))
     short_total, medium_total = ctx_totals(shares)
     (mr_out,) = blocks_call(
         "mr_backward",
         mr_backward_kernel,
         [v2, v2_ahead, w2, product, mf, rate, behind, product_ahead, g, ahead, mw],
         [fwd, rim, inv],
-        [((2, rows), BF16)],
+        [((rows, 2), BF16)],
         [
             bf16_rows(256),
             pltpu.VMEM((end, BLOCK), F32),
@@ -608,7 +617,7 @@
     )
     return (
         jnp.transpose(se_out, (1, 0, 2)),
-        jnp.transpose(mr_out, (1, 0, 2)),
+        mr_out,
         short_total,
         medium_total,
     )

time: 86 us -> 83 us (0.965)
  local copies, waits for them, and re-layouts: 12.4 us -> 3.62 us
  Pallas kernels: 31.9 us -> 37.9 us
  starting transfers between devices: 29.5 us -> 31.1 us
  other arithmetic: 1.26 us -> 0.27 us
    unnamed x8 -> x10, local copies, waits for them, and re-layouts: 6.48 us -> 1.38 us
    pallas_call x4, Pallas kernels: 29.6 us -> 33.4 us  [blocks_call(): pl.pallas_call(body, grid=(channels // BLOCK,), in_specs=[rows_of(*a.shap...]
    all_to_all x2, starting transfers between devices: 20.2 us -> 23.1 us  [the longest x1 14.2 us: local(): shares = lax.all_to_all(terms, 'ctx', 0, 0, tiled=True)]
    ppermute x1, waiting for transfers between devices: 0.01 us -> 2.35 us  [local(): ahead = lax.ppermute(first, 'ctx', backward)]
    pallas_call x1 -> x2, Pallas kernels: 2.31 us -> 4.57 us  [edge_call(): pl.pallas_call(body, grid=(channels // wide,), in_specs=[pairs(count, at)...]
    ppermute x1, waiting for transfers between devices: 2.2 us -> 0.01 us  [local(): before = lax.ppermute(last, 'ctx', onward)]
    reshape x2 -> x0, local copies, waits for them, and re-layouts: 1.96 us -> none  [the longest x1 1.14 us: ctx_shares(): medium_part.reshape(count, depth, -1)]
    slice x3 -> x1, local copies, waits for them, and re-layouts: 1.71 us -> 0.02 us  [ctx_totals(): short_total = totals[:channels // 16, 0, channels:].reshape(-1, 8, LANES)]
  transfers between devices with their start and end apart: 5 -> 5, of which waited for: 2 -> 4; matrix products, arithmetic and copies ran while one was open for 6% -> 0% of each run, Pallas kernels for 35% -> 32%
where the time goes in v2:
time: 83 us; the launch traced here: 82.5 us
  Pallas kernels  37.9 us (46%)
  starting transfers between devices  31.1 us (37%)
  waiting for transfers between devices  8.85 us (11%)
  local copies, waits for them, and re-layouts  3.62 us (4%)
    pallas_call x4, Pallas kernels, blocks_call(): pl.pallas_call(body, grid=(channels // BLOCK,), in_specs=[rows_of(*a.shap...  33.4 us
    all_to_all x1, starting transfers between devices, local(): shares = lax.all_to_all(terms, 'ctx', 0, 0, tiled=True)  14.2 us
    all_to_all x1, starting transfers between devices, ctx_totals(): lax.all_to_all(copies, 'ctx', 0, 0, tiled=True).reshape(64, 2, width)  8.91 us
    pallas_call x2, Pallas kernels, edge_call(): pl.pallas_call(body, grid=(channels // wide,), in_specs=[pairs(count, at)...  4.57 us
    all_to_all x1, waiting for transfers between devices, local(): shares = lax.all_to_all(terms, 'ctx', 0, 0, tiled=True)  3.7 us
    ppermute x1, starting transfers between devices, local(): behind = lax.ppermute(edge, 'ctx', onward)  3.49 us
    ppermute x1, starting transfers between devices, local(): before = lax.ppermute(last, 'ctx', onward)  3.18 us
    ppermute x1, waiting for transfers between devices, local(): ahead = lax.ppermute(first, 'ctx', backward)  2.35 us
  transfers between devices with their start and end apart: 5, of which 4 were waited for; matrix products, arithmetic and copies ran while one was open for 0% of the time, Pallas kernels for 32%

profile of v2, /device:TPU:16, one launch (start us, length us, event | category | flops | bytes accessed | tf_op | source)
XLA Modules:
  0.0 82.5 jit_solution(13446531031814104996)
XLA Ops:
  0.6 1.8 %last_rows.1.after_ref.last_ref = bf16[32,1024]{1,0:T(8,128)(2,1)} custom-call(bf16[3,256,1024]{2,1,0:T(8,128)(2,1)} %bitcast.12, bf16[256,2,1024]{2,1,0:T(2,128)(2,1)} %mr_ref.1, f32[3,3,1024]{2,1,0:T(4,128)} %sw_ref.7, f32[7,1024]{1,0:T(8,128)} %sf_ref.7), custom_call_target="tpu_custom_call" | custom-call | tf_op jit(solution)/shard_map/last_rows/pallas_call | solution.py:474
  2.5 3.2 %collective-permute-start = (bf16[32,1024]{1,0:T(8,128)(2,1)}, bf16[32,1024]{1,0:T(8,128)(2,1)S(1)}, u32[]{:S(2)}, u32[]{:S(2)}) collective-permute-start(bf16[32,1024]{1,0:T(8,128)(2,1)} %last_rows.1.after_ref.last_ref), channel_id=1, source_target_pairs={{0,4},{4,8},{8,12},{12,16},{16,20},{20,24},{24,28},{28,32},{32,36}... | collective-permute-start | bytes 196616 | tf_op jit(solution)/shard_map/ppermute | solution.py:533
  5.7 2.7 %first_rows.1 = bf16[176,1024]{1,0:T(8,128)(2,1)} custom-call(bf16[3,256,1024]{2,1,0:T(8,128)(2,1)} %bitcast.13, bf16[256,2,1024]{2,1,0:T(2,128)(2,1)} %mr_ref.1, bf16[256,1024]{1,0:T(8,128)(2,1)} %g_ref.5, f32[3,3,1024]{2,1,0:T(4,128)} %mw_ref.7, bf16[32,1024]{1,0:T(8,128)(2,1)} %last_rows.1.after_ref.last_ref), custom_call_target="tpu_custom_call" | custom-call | tf_op jit(solution)/shard_map/first_rows/pallas_call | solution.py:474
  8.4 0.0 collective-permute-done.before_ref
  8.4 0.0 copy-start.1
  8.4 1.3 %collective-permute-start.1 = (bf16[176,1024]{1,0:T(8,128)(2,1)}, bf16[176,1024]{1,0:T(8,128)(2,1)S(1)}, u32[]{:S(2)}, u32[]{:S(2)}) collective-permute-start(bf16[176,1024]{1,0:T(8,128)(2,1)} %first_rows.1), channel_id=1, source_target_pairs={{4,0},{8,4},{12,8},{16,12},{20,16},{24,20},{28,24},{32,28},{36,32}... | collective-permute-start | bytes 1081352 | tf_op jit(solution)/shard_map/ppermute | solution.py:535
  9.7 0.0 copy-done.1
  9.7 8.7 %forward.1 = (f32[256,1024]{1,0:T(8,128)}, f32[256,1024]{1,0:T(8,128)}, f32[256,1024]{1,0:T(8,128)}, f32[256,1024]{1,0:T(8,128)}, bf16[256,1024]{1,0:T(8,128)(2,...) custom-call(bf16[3,256,1024]{2,1,0:T(8,128)(2,1)} %bitcast.14, ...), custom_call_target="tpu_custom_call" | custom-call | flops 1048576000 | bytes 4194304 | tf_op jit(solution)/shard_map/forward/pallas_call | solution.py:447
  18.4 2.4 %collective-permute-done.1.ahead_ref = bf16[176,1024]{1,0:T(8,128)(2,1)S(1)} collective-permute-done((bf16[176,1024]{1,0:T(8,128)(2,1)}, bf16[176,1024]{1,0:T(8,128)(2,1)S(1)}, u32[]{:S(2)}, u32[]{:S(2)}) %collective-permute-start.1) | collective-permute-done | bytes 360480 | tf_op jit(solution)/shard_map/ppermute | solution.py:535
  20.7 0.0 copy-start
  20.7 0.7 copy-done
  21.5 0.0 copy-start.3
  21.5 9.3 %middle.1 = (f32[272,1024]{1,0:T(8,128)}, f32[272,1024]{1,0:T(8,128)}, f32[5,16,1024]{2,1,0:T(8,128)}, f32[16,1024]{1,0:T(8,128)}, bf16[16,1024]{1,0:T(8,128)(2,1)}, /*index=5*/bf16[64,2,1152]{2,1,0:T(2,128)(2,1)}) custom-call(f32[256,1024]{1,0:T(8,128)} %get-tuple-element.26.q1_ref, f32[256,1024]{1,0:T(8,128)} %get-tuple-element.27.k2_ref, ...), custom_call_target="tpu_custom_call" | custom-call | flops 1048576000 | bytes 4194304 | tf_op jit(solution)/shard_map/middle/pallas_call | solution.py:447
  30.8 14.2 %all-to-all-start = ((bf16[64,2,1152]{2,1,0:T(2,128)(2,1)}), bf16[64,2,1152]{2,1,0:T(2,128)(2,1)S(1)}, u32[]{:S(2)}, u32[]{:S(2)}) async-start(bf16[64,2,1152]{2,1,0:T(2,128)(2,1)} %get-tuple-element.34), calls=%async_computation | async-start | bytes 589824 | tf_op jit(solution)/shard_map/all_to_all | solution.py:587
  45.0 0.0 copy-done.3
  45.0 3.5 %collective-permute-start.2 = (bf16[128,1024]{1,0:T(8,128)(2,1)S(1)}, bf16[128,1024]{1,0:T(8,128)(2,1)S(1)}, u32[]{:S(2)}, u32[]{:S(2)}) collective-permute-start(bf16[128,1024]{1,0:T(8,128)(2,1)S(1)} %copy-done.3), channel_id=1, source_target_pairs={{0,4},{4,8},{8,12},{12,16},{16,20},{20,24},{24,28},{28,32},{32,36}... | collective-permute-start | bytes 786440 | tf_op jit(solution)/shard_map/ppermute | solution.py:585
  48.5 5.1 %se_backward.1 = bf16[3,256,1024]{2,1,0:T(8,128)(2,1)} custom-call(f32[256,1024]{1,0:T(8,128)} %get-tuple-element.26.q1_ref, f32[256,1024]{1,0:T(8,128)} %get-tuple-element.35.z1_ref, f32[5,16,1024]{2,1,0:T(8,128)} %get-tuple-element.36.feats_ahead, f32[272,1024]{1,0:T(8,128)} %get-tuple-element.37.dy1, bf16[3,256,1024]{2,1,0:T(8,128)(2,1)} %bitcast.15, ...), custom_call_target="tpu_custom_call" | custom-call | flops 524288000 | bytes 4194304 | tf_op jit(solution)/shard_map/se_backward/pallas_call | solution.py:447
  53.6 1.0 %collective-permute-done.2.behind_ref = bf16[128,1024]{1,0:T(8,128)(2,1)S(1)} collective-permute-done((bf16[128,1024]{1,0:T(8,128)(2,1)S(1)}, bf16[128,1024]{1,0:T(8,128)(2,1)S(1)}, u32[]{:S(2)}, u32[]{:S(2)}) %collective-permute-start.2) | collective-permute-done | bytes 262176 | tf_op jit(solution)/shard_map/ppermute | solution.py:585
  54.7 0.0 copy-start.2
  54.7 3.7 %all-to-all-done = bf16[64,2,1152]{2,1,0:T(2,128)(2,1)S(1)} async-done(((bf16[64,2,1152]{2,1,0:T(2,128)(2,1)}), bf16[64,2,1152]{2,1,0:T(2,128)(2,1)S(1)}, u32[]{:S(2)}, u32[]{:S(2)}) %all-to-all-start) | async-done | bytes 294944 | tf_op jit(solution)/shard_map/all_to_all | solution.py:587
  58.4 0.3 reduce_sum.12
  58.6 0.9 %broadcast_in_dim.10 = bf16[64,2,1152]{2,1,0:T(2,128)(2,1)} broadcast(bf16[2,1152]{1,0:T(2,128)(2,1)S(1)} %reduce_sum.12), dimensions={1,2} | broadcast | bytes 299520 | tf_op jit(solution)/shard_map/broadcast_in_dim | solution.py:512
  59.5 8.9 %all-to-all-start.1 = ((bf16[64,2,1152]{2,1,0:T(2,128)(2,1)}), bf16[64,2,1152]{2,1,0:T(2,128)(2,1)S(1)}, u32[]{:S(2)}, u32[]{:S(2)}) async-start(bf16[64,2,1152]{2,1,0:T(2,128)(2,1)} %broadcast_in_dim.10), calls=%async_computation.1 | async-start | bytes 589824 | tf_op jit(solution)/shard_map/all_to_all | solution.py:513
  68.4 0.0 copy-done.2
  68.4 10.3 %mr_backward.1 = bf16[256,2,1024]{2,1,0:T(2,128)(2,1)} custom-call(f32[256,1024]{1,0:T(8,128)} %get-tuple-element.40.v2, f32[16,1024]{1,0:T(8,128)} %get-tuple-element.41.v2_ahead, f32[272,1024]{1,0:T(8,128)} %get-tuple-element.42.w2, bf16[256,1024]{1,0:T(8,128)(2,1)} %get-tuple-element.29.pb.own_ref, f32[128,1024]{1,0:T(8,128)} %mf_ref.3, ...), custom_call_target="tpu_custom_call" | custom-call | flops 524288000 | bytes 4194304 | tf_op jit(solution)/shard_map/mr_backward/pallas_call | solution.py:447
  78.7 1.8 %all-to-all-done.1 = bf16[64,2,1152]{2,1,0:T(2,128)(2,1)S(1)} async-done(((bf16[64,2,1152]{2,1,0:T(2,128)(2,1)}), bf16[64,2,1152]{2,1,0:T(2,128)(2,1)S(1)}, u32[]{:S(2)}, u32[]{:S(2)}) %all-to-all-start.1) | async-done | bytes 294944 | tf_op jit(solution)/shard_map/all_to_all | solution.py:513
  80.5 0.6 copy.19
  81.1 0.2 slice.18
  81.3 1.2 %reshape.14 = f32[128,1024]{1,0:T(8,128)} reshape(f32[64,2,1024]{2,1,0:T(2,128)S(1)} %slice.18) | data formatting | bytes 1048576 | tf_op jit(solution)/shard_map/reshape | solution.py:514
  (3 shorter events, 0.0 us)
Async XLA Ops:
  2.5 5.9 %collective-permute-start = (bf16[32,1024]{1,0:T(8,128)(2,1)}, bf16[32,1024]{1,0:T(8,128)(2,1)S(1)}, u32[]{:S(2)}, u32[]{:S(2)}) collective-permute-start(bf16[32,1024]{1,0:T(8,128)(2,1)} %last_rows.1.after_ref.last_ref), channel_id=1, source_target_pairs={{0,4},{4,8},{8,12},{12,16},{16,20},{20,24},{24,28},{28,32},{32,36}... | collective-permute-start | bytes 196616 | tf_op jit(solution)/shard_map/ppermute | solution.py:533
  8.4 1.3 %copy-start.1 = (bf16[32,1024]{1,0:T(8,128)(2,1)}, bf16[32,1024]{1,0:T(8,128)(2,1)S(1)}, u32[]{:S(2)}) copy-start(bf16[32,1024]{1,0:T(8,128)(2,1)S(1)} %collective-permute-done.before_ref) | copy-start | bytes 196612
  8.4 12.3 %collective-permute-start.1 = (bf16[176,1024]{1,0:T(8,128)(2,1)}, bf16[176,1024]{1,0:T(8,128)(2,1)S(1)}, u32[]{:S(2)}, u32[]{:S(2)}) collective-permute-start(bf16[176,1024]{1,0:T(8,128)(2,1)} %first_rows.1), channel_id=1, source_target_pairs={{4,0},{8,4},{12,8},{16,12},{20,16},{24,20},{28,24},{32,28},{36,32}... | collective-permute-start | bytes 1081352 | tf_op jit(solution)/shard_map/ppermute | solution.py:535
  20.7 0.7 copy-start
  21.5 23.5 %copy-start.3 = (bf16[128,1024]{1,0:T(8,128)(2,1)S(1)}, bf16[128,1024]{1,0:T(8,128)(2,1)}, u32[]{:S(2)}) copy-start(bf16[128,1024]{1,0:T(8,128)(2,1)} %get-tuple-element.38) | copy-start | bytes 786436
  30.8 27.6 %all-to-all-start = ((bf16[64,2,1152]{2,1,0:T(2,128)(2,1)}), bf16[64,2,1152]{2,1,0:T(2,128)(2,1)S(1)}, u32[]{:S(2)}, u32[]{:S(2)}) async-start(bf16[64,2,1152]{2,1,0:T(2,128)(2,1)} %get-tuple-element.34), calls=%async_computation | async-start | bytes 589824 | tf_op jit(solution)/shard_map/all_to_all | solution.py:587
  45.0 9.6 %collective-permute-start.2 = (bf16[128,1024]{1,0:T(8,128)(2,1)S(1)}, bf16[128,1024]{1,0:T(8,128)(2,1)S(1)}, u32[]{:S(2)}, u32[]{:S(2)}) collective-permute-start(bf16[128,1024]{1,0:T(8,128)(2,1)S(1)} %copy-done.3), channel_id=1, source_target_pairs={{0,4},{4,8},{8,12},{12,16},{16,20},{20,24},{24,28},{28,32},{32,36}... | collective-permute-start | bytes 786440 | tf_op jit(solution)/shard_map/ppermute | solution.py:585
  54.7 13.8 %copy-start.2 = (bf16[128,1024]{1,0:T(8,128)(2,1)}, bf16[128,1024]{1,0:T(8,128)(2,1)S(1)}, u32[]{:S(2)}) copy-start(bf16[128,1024]{1,0:T(8,128)(2,1)S(1)} %collective-permute-done.2.behind_ref) | copy-start | bytes 786436
  59.5 21.0 %all-to-all-start.1 = ((bf16[64,2,1152]{2,1,0:T(2,128)(2,1)}), bf16[64,2,1152]{2,1,0:T(2,128)(2,1)S(1)}, u32[]{:S(2)}, u32[]{:S(2)}) async-start(bf16[64,2,1152]{2,1,0:T(2,128)(2,1)} %broadcast_in_dim.10), calls=%async_computation.1 | async-start | bytes 589824 | tf_op jit(solution)/shard_map/all_to_all | solution.py:513

commit v3 on v2

--- a/solution.py
+++ b/solution.py
@@ -117,13 +117,15 @@
         last_ref[:, lanes] = tail[...].astype(BF16)
 
 
-def first_kernel(se_start, mr_start, g_ref, mw_ref, after_ref, first_ref, x, y1, tail):
+def first_kernel(se_start, mr_start, g_ref, mw_ref, after_ref, first_ref, x, y1, tail, pairs):
     for h in range(g_ref.shape[1] // LANES):
         lanes = lanes_of(h)
         mw = feature_taps(mw_ref, lanes)
         x[3, 0:PAD, :] = jnp.zeros((PAD, LANES), F32)
         for a, n in chunks(0, 144):
-            x[3, pl.ds(PAD + a, n), :] = mr_start[pl.ds(a, n), 0, lanes].astype(F32)
+            both = mr_start[pl.ds(a, n), :, lanes].reshape(2 * n, LANES)
+            pairs[pl.ds(2 * a, 2 * n), :] = both.astype(F32)
+            x[3, pl.ds(PAD + a, n), :] = pairs[pl.ds(2 * a, n, 2), :]
         for a, n in chunks(0, 144):
             q2 = weighted(x, (3,), PAD + a, n, mw[0], -1)
             first_ref[pl.ds(a, n), lanes] = (
@@ -131,7 +133,7 @@
             ).astype(BF16)
         for p in range(3):
             x[p, 0:16, :] = se_start[p, :, lanes].astype(F32)
-        x[4, 0:16, :] = mr_start[0:16, 1, lanes].astype(F32)
+        x[4, 0:16, :] = pairs[pl.ds(1, 16, 2), :]
         y1[0:16, :] = g_ref[0:16, lanes].astype(F32)
         tail[...] = jnp.zeros((32, LANES), F32)
         tail[0:2, :] = y1[0:2, :]
@@ -171,6 +173,7 @@
     y1,
     tail,
     db,
+    pairs,
 ):
     rows = se_ref.shape[1]
     for h in range(BLOCK // LANES):
@@ -186,8 +189,10 @@
         for t, n in chunks(0, rows):
             for p in range(3):
                 x[p, pl.ds(PAD + t, n), :] = se_ref[p, pl.ds(t, n), lanes].astype(F32)
+            both = mr_ref[pl.ds(t, n), :, lanes].reshape(2 * n, LANES)
+            pairs[pl.ds(2 * t, 2 * n), :] = both.astype(F32)
             for p in range(2):
-                x[3 + p, pl.ds(PAD + t, n), :] = mr_ref[pl.ds(t, n), p, lanes].astype(F32)
+                x[3 + p, pl.ds(PAD + t, n), :] = pairs[pl.ds(2 * t + p, n, 2), :]
         for t, n in chunks(0, rows):
             r, at = PAD + t, pl.ds(t, n)
             key = weighted(x, (1,), r, n, sw[1], -1)
@@ -341,13 +346,32 @@
 
 
 def se_backward_kernel(
-    q1_ref, z1_ref, feats_ahead, dy1, se_ref, before_ref, sw_ref, sf_ref, se_out, x, tail, e, dz
+    q1_ref,
+    z1_ref,
+    feats_ahead,
+    v2,
+    v2_ahead,
+    w2,
+    dy1,
+    se_ref,
+    before_ref,
+    sw_ref,
+    mw_ref,
+    sf_ref,
+    se_out,
+    key_out,
+    x,
+    tail,
+    d,
+    e,
+    dz,
 ):
     rows = q1_ref.shape[0]
     for h in range(BLOCK // LANES):
         lanes = lanes_of(h)
         sw = feature_taps(sw_ref, lanes)
         sf = short_taps(sf_ref, lanes)
+        key_taps = [mw_ref[j, 1, lanes][None, :] for j in range(3)]
         tail[...] = before_ref[:, lanes].astype(F32)
         for p in range(2):
             x[p, PAD - 2 : PAD, :] = tail[10 + 2 * p : 12 + 2 * p, :]
@@ -355,6 +379,8 @@
                 x[p, pl.ds(PAD + t, n), :] = se_ref[1 + p, pl.ds(t, n), lanes].astype(F32)
         for base, t, n in spans(rows):
             at, own = pl.ds(t, n), pl.ds(t - base, n)
+            value = v2_ahead[own, lanes] if base else v2[own, lanes]
+            d[at, :] = w2[at, lanes] * value
             grad = dy1[at, lanes]
             query = feats_ahead[0, own, lanes] if base else q1_ref[own, lanes]
             mixed = feats_ahead[1, own, lanes] if base else z1_ref[own, lanes]
@@ -374,12 +400,11 @@
             at = pl.ds(t, n)
             for p in range(3):
                 se_out[p, at, lanes] = weighted(e, (p,), t, n, sw[p], 1).astype(BF16)
+            key_out[at, lanes] = weighted(d, (), t, n, key_taps, 1).astype(BF16)
 
 
 def mr_backward_kernel(
-    v2,
-    v2_ahead,
-    w2,
+    key_grad,
     own_ref,
     mf_ref,
     rate_ref,
@@ -396,8 +421,9 @@
     z2,
     tail,
     d,
+    pairs,
 ):
-    rows = v2.shape[0]
+    rows = key_grad.shape[0]
     pb[0:128, :] = behind_ref[...]
     pb[128 : 128 + REACH, :] = product_ref[...]
     pb[128 + REACH : 256, :] = jnp.zeros((128 - REACH, BLOCK), BF16)
@@ -416,14 +442,15 @@
         tail[...] = ahead_ref[144:176, lanes].astype(F32)
         tail[2:16, :] = jnp.zeros((14, LANES), F32)
         for base, t, n in spans(rows):
-            at, own = pl.ds(t, n), pl.ds(t - base, n)
-            value = v2_ahead[own, lanes] if base else v2[own, lanes]
-            d[1, at, :] = w2[at, lanes] * value
+            at = pl.ds(t, n)
             upstream = tail[0:REACH, :] if base else g_ref[at, lanes].astype(F32)
-            d[0, at, :] = upstream * z2[at, lanes]
+            d[at, :] = upstream * z2[at, lanes]
         for t, n in chunks(0, rows):
-            pair = [weighted(d, (p,), t, n, mw[p], 1)[:, None, :] for p in range(2)]
-            mr_out[pl.ds(t, n), :, lanes] = jnp.concatenate(pair, axis=1).astype(BF16)
+            at = pl.ds(t, n)
+            pairs[pl.ds(2 * t, n, 2), :] = weighted(d, (), t, n, mw[0], 1)
+            pairs[pl.ds(2 * t + 1, n, 2), :] = key_grad[at, lanes].astype(F32)
+            both = pairs[pl.ds(2 * t, 2 * n), :].astype(BF16)
+            mr_out[at, :, lanes] = both.reshape(n, 2, LANES)
 
 
 def rows_of(*dims):
@@ -442,7 +469,7 @@
     return pltpu.VMEM(dims + (BLOCK,), BF16)
 
 
-def blocks_call(name, body, arrays, tables, outs, scratch, flops, whole=()):
+def blocks_call(name, body, arrays, tables, outs, scratch, flops, whole=(), limit=LIMIT):
     channels = arrays[0].shape[-1]
     return pl.pallas_call(
         body,
@@ -452,7 +479,7 @@
         out_shape=[jax.ShapeDtypeStruct(dims + (channels,), kind) for dims, kind in outs]
         + list(whole),
         scratch_shapes=scratch,
-        compiler_params=pltpu.CompilerParams(vmem_limit_bytes=LIMIT),
+        compiler_params=pltpu.CompilerParams(vmem_limit_bytes=limit),
         cost_estimate=pl.CostEstimate(
             flops=flops * 256 * channels, bytes_accessed=16 * 256 * channels, transcendentals=0
         ),
@@ -500,21 +527,22 @@
         first_kernel,
         [(se, 16, 0), (mr, 144, 0), (g, 144, 0), (mw, 3, 0), (last, 32, 0)],
         176,
-        [f32_rows(5, 160), f32_rows(32), f32_rows(32)],
+        [f32_rows(5, 160), f32_rows(32), f32_rows(32), f32_rows(288)],
     )
     return last, first
 
 
-def ctx_totals(shares):
+def ctx_totals(shares, behind):
     count, depth, width = shares.shape
     channels = width - LANES
     total = jnp.sum(shares.astype(F32), axis=0).astype(BF16)
     copies = jnp.broadcast_to(total[None], shares.shape)
+    copies, behind = lax.optimization_barrier((copies, behind))
     totals = lax.all_to_all(copies, "ctx", 0, 0, tiled=True).reshape(64, 2, width).astype(F32)
     medium_total = totals[:, :, :channels].reshape(count * depth, channels)
     short_total = totals[: channels // 16, 0, channels:].reshape(-1, 8, LANES)
     short_total = jnp.swapaxes(short_total, 0, 1).reshape(8, channels)[:7]
-    return short_total, medium_total
+    return short_total, medium_total, behind
 
 
 def local(tables, se_input, mr_input, g, sw, mw, sf, mf, decay_rate):
@@ -554,6 +582,7 @@
             f32_rows(PAD + rows),
             f32_rows(32),
             bf16_rows(2, rows),
+            f32_rows(2 * rows),
         ],
         4000,
     )
@@ -585,33 +614,35 @@
     behind = lax.ppermute(edge, "ctx", onward)
     terms = terms.reshape(count, 128 // count, channels + LANES)
     shares = lax.all_to_all(terms, "ctx", 0, 0, tiled=True)
-    (se_out,) = blocks_call(
+    se_out, key_grad = blocks_call(
         "se_backward",
         se_backward_kernel,
-        [q1, z1, feats_ahead, dy1, se, before, sw, sf],
+        [q1, z1, feats_ahead, v2, v2_ahead, w2, dy1, se, before, sw, mw, sf],
         [],
-        [((3, rows), BF16)],
+        [((3, rows), BF16), ((rows,), BF16)],
         [
             f32_rows(2, PAD + rows),
             f32_rows(32),
+            f32_rows(end + 16),
             f32_rows(3, end + 16),
             f32_rows(end + 16),
         ],
         2000,
     )
-    shares, se_out, behind = lax.optimization_barrier((shares, se_out, behind))
-    short_total, medium_total = ctx_totals(shares)
+    shares, key_grad = lax.optimization_barrier((shares, key_grad))
+    short_total, medium_total, behind = ctx_totals(shares, behind)
     (mr_out,) = blocks_call(
         "mr_backward",
         mr_backward_kernel,
-        [v2, v2_ahead, w2, product, mf, rate, behind, product_ahead, g, ahead, mw],
+        [key_grad, product, mf, rate, behind, product_ahead, g, ahead, mw],
         [fwd, rim, inv],
         [((rows, 2), BF16)],
         [
             bf16_rows(256),
             pltpu.VMEM((end, BLOCK), F32),
             f32_rows(32),
-            f32_rows(2, end + 16),
+            f32_rows(end + 16),
+            f32_rows(2 * rows),
         ],
         2000,
     )

time: 83 us -> 82.4 us (level)
  Pallas kernels: 37.9 us -> 36.1 us
  waiting for transfers between devices: 8.85 us -> 10.5 us
    pallas_call x4, Pallas kernels: 33.4 us -> 31.8 us  [blocks_call(): pl.pallas_call(body, grid=(channels // BLOCK,), in_specs=[rows_of(*a.shap...]
    all_to_all x1, waiting for transfers between devices: 1.77 us -> 3.23 us  [ctx_totals(): lax.all_to_all(copies, 'ctx', 0, 0, tiled=True).reshape(64, 2, width)]
    ppermute x1, waiting for transfers between devices: 1.02 us -> 0.01 us  [local(): behind = lax.ppermute(edge, 'ctx', onward)]
    ppermute x1, waiting for transfers between devices: 2.35 us -> 3.31 us  [local(): ahead = lax.ppermute(first, 'ctx', backward)]
  transfers between devices with their start and end apart: 5 -> 5, of which waited for: 4 -> 3; matrix products, arithmetic and copies ran while one was open for 0% -> 0% of each run, Pallas kernels for 32% -> 31%
where the time goes in v3:
time: 82.4 us; the launch traced here: 81.9 us
  Pallas kernels  36.1 us (44%)
  starting transfers between devices  30.6 us (37%)
  waiting for transfers between devices  10.5 us (13%)
  local copies, waits for them, and re-layouts  3.6 us (4%)
    pallas_call x4, Pallas kernels, blocks_call(): pl.pallas_call(body, grid=(channels // BLOCK,), in_specs=[rows_of(*a.shap...  31.8 us
    all_to_all x1, starting transfers between devices, local(): shares = lax.all_to_all(terms, 'ctx', 0, 0, tiled=True)  13.9 us
    all_to_all x1, starting transfers between devices, ctx_totals(): lax.all_to_all(copies, 'ctx', 0, 0, tiled=True).reshape(64, 2, width)  8.76 us
    pallas_call x2, Pallas kernels, edge_call(): pl.pallas_call(body, grid=(channels // wide,), in_specs=[pairs(count, at)...  4.3 us
    all_to_all x1, waiting for transfers between devices, local(): shares = lax.all_to_all(terms, 'ctx', 0, 0, tiled=True)  4 us
    ppermute x1, starting transfers between devices, local(): behind = lax.ppermute(edge, 'ctx', onward)  3.49 us
    ppermute x1, waiting for transfers between devices, local(): ahead = lax.ppermute(first, 'ctx', backward)  3.31 us
    all_to_all x1, waiting for transfers between devices, ctx_totals(): lax.all_to_all(copies, 'ctx', 0, 0, tiled=True).reshape(64, 2, width)  3.23 us
  transfers between devices with their start and end apart: 5, of which 3 were waited for; matrix products, arithmetic and copies ran while one was open for 0% of the time, Pallas kernels for 31%

profile of v3, /device:TPU:16, one launch (start us, length us, event | category | flops | bytes accessed | tf_op | source)
XLA Modules:
  0.0 81.9 jit_solution(3405674067658204931)
XLA Ops:
  0.6 1.8 %last_rows.1.after_ref.last_ref = bf16[32,1024]{1,0:T(8,128)(2,1)} custom-call(bf16[3,256,1024]{2,1,0:T(8,128)(2,1)} %bitcast.12, bf16[256,2,1024]{2,1,0:T(2,128)(2,1)} %mr_ref.1, f32[3,3,1024]{2,1,0:T(4,128)} %sw_ref.7, f32[7,1024]{1,0:T(8,128)} %sf_ref.7), custom_call_target="tpu_custom_call" | custom-call | tf_op jit(solution)/shard_map/last_rows/pallas_call | solution.py:501
  2.5 3.2 %collective-permute-start = (bf16[32,1024]{1,0:T(8,128)(2,1)}, bf16[32,1024]{1,0:T(8,128)(2,1)S(1)}, u32[]{:S(2)}, u32[]{:S(2)}) collective-permute-start(bf16[32,1024]{1,0:T(8,128)(2,1)} %last_rows.1.after_ref.last_ref), channel_id=1, source_target_pairs={{0,4},{4,8},{8,12},{12,16},{16,20},{20,24},{24,28},{28,32},{32,36}... | collective-permute-start | bytes 196616 | tf_op jit(solution)/shard_map/ppermute | solution.py:561
  5.7 2.5 %first_rows.1 = bf16[176,1024]{1,0:T(8,128)(2,1)} custom-call(bf16[3,256,1024]{2,1,0:T(8,128)(2,1)} %bitcast.13, bf16[256,2,1024]{2,1,0:T(2,128)(2,1)} %mr_ref.1, bf16[256,1024]{1,0:T(8,128)(2,1)} %g_ref.5, f32[3,3,1024]{2,1,0:T(4,128)} %mw_ref.9, bf16[32,1024]{1,0:T(8,128)(2,1)} %last_rows.1.after_ref.last_ref), custom_call_target="tpu_custom_call" | custom-call | tf_op jit(solution)/shard_map/first_rows/pallas_call | solution.py:501
  8.1 0.0 collective-permute-done.before_ref
  8.1 0.0 copy-start.1
  8.1 1.3 %collective-permute-start.1 = (bf16[176,1024]{1,0:T(8,128)(2,1)}, bf16[176,1024]{1,0:T(8,128)(2,1)S(1)}, u32[]{:S(2)}, u32[]{:S(2)}) collective-permute-start(bf16[176,1024]{1,0:T(8,128)(2,1)} %first_rows.1), channel_id=1, source_target_pairs={{4,0},{8,4},{12,8},{16,12},{20,16},{24,20},{28,24},{32,28},{36,32}... | collective-permute-start | bytes 1081352 | tf_op jit(solution)/shard_map/ppermute | solution.py:563
  9.4 0.0 copy-done.1
  9.4 7.7 %forward.1 = (f32[256,1024]{1,0:T(8,128)}, f32[256,1024]{1,0:T(8,128)}, f32[256,1024]{1,0:T(8,128)}, f32[256,1024]{1,0:T(8,128)}, bf16[256,1024]{1,0:T(8,128)(2,...) custom-call(bf16[3,256,1024]{2,1,0:T(8,128)(2,1)} %bitcast.14, ...), custom_call_target="tpu_custom_call" | custom-call | flops 1048576000 | bytes 4194304 | tf_op jit(solution)/shard_map/forward/pallas_call | solution.py:474
  17.1 3.3 %collective-permute-done.1.ahead_ref = bf16[176,1024]{1,0:T(8,128)(2,1)S(1)} collective-permute-done((bf16[176,1024]{1,0:T(8,128)(2,1)}, bf16[176,1024]{1,0:T(8,128)(2,1)S(1)}, u32[]{:S(2)}, u32[]{:S(2)}) %collective-permute-start.1) | collective-permute-done | bytes 360480 | tf_op jit(solution)/shard_map/ppermute | solution.py:563
  20.5 0.0 copy-start
  20.5 0.7 copy-done
  21.2 0.0 copy-start.3
  21.2 9.3 %middle.1 = (f32[272,1024]{1,0:T(8,128)}, f32[272,1024]{1,0:T(8,128)}, f32[5,16,1024]{2,1,0:T(8,128)}, f32[16,1024]{1,0:T(8,128)}, bf16[16,1024]{1,0:T(8,128)(2,1)}, /*index=5*/bf16[64,2,1152]{2,1,0:T(2,128)(2,1)}) custom-call(f32[256,1024]{1,0:T(8,128)} %get-tuple-element.29.q1_ref, f32[256,1024]{1,0:T(8,128)} %get-tuple-element.31.k2_ref, ...), custom_call_target="tpu_custom_call" | custom-call | flops 1048576000 | bytes 4194304 | tf_op jit(solution)/shard_map/middle/pallas_call | solution.py:474
  30.5 13.9 %all-to-all-start = ((bf16[64,2,1152]{2,1,0:T(2,128)(2,1)}), bf16[64,2,1152]{2,1,0:T(2,128)(2,1)S(1)}, u32[]{:S(2)}, u32[]{:S(2)}) async-start(bf16[64,2,1152]{2,1,0:T(2,128)(2,1)} %get-tuple-element.44), calls=%async_computation | async-start | bytes 589824 | tf_op jit(solution)/shard_map/all_to_all | solution.py:616
  44.4 0.0 copy-done.3
  44.4 3.5 %collective-permute-start.2 = (bf16[128,1024]{1,0:T(8,128)(2,1)S(1)}, bf16[128,1024]{1,0:T(8,128)(2,1)S(1)}, u32[]{:S(2)}, u32[]{:S(2)}) collective-permute-start(bf16[128,1024]{1,0:T(8,128)(2,1)S(1)} %copy-done.3), channel_id=1, source_target_pairs={{0,4},{4,8},{8,12},{12,16},{16,20},{20,24},{24,28},{28,32},{32,36}... | collective-permute-start | bytes 786440 | tf_op jit(solution)/shard_map/ppermute | solution.py:614
  47.9 5.9 %se_backward.1 = (bf16[3,256,1024]{2,1,0:T(8,128)(2,1)}, bf16[256,1024]{1,0:T(8,128)(2,1)}) custom-call(f32[256,1024]{1,0:T(8,128)} %get-tuple-element.29.q1_ref, f32[256,1024]{1,0:T(8,128)} %get-tuple-element.30.z1_ref, f32[5,16,1024]{2,1,0:T(8,128)} %get-tuple-element.36.feats_ahead, f32[256,1024]{1,0:T(8,128)} %get-tuple-element.37.v2, ...), custom_call_target="tpu_custom_call" | custom-call | flops 524288000 | bytes 4194304 | tf_op jit(solution)/shard_map/se_backward/pallas_call | solution.py:474
  53.8 4.0 %all-to-all-done = bf16[64,2,1152]{2,1,0:T(2,128)(2,1)S(1)} async-done(((bf16[64,2,1152]{2,1,0:T(2,128)(2,1)}), bf16[64,2,1152]{2,1,0:T(2,128)(2,1)S(1)}, u32[]{:S(2)}, u32[]{:S(2)}) %all-to-all-start) | async-done | bytes 294944 | tf_op jit(solution)/shard_map/all_to_all | solution.py:616
  57.8 0.3 reduce_sum.12
  58.1 0.0 collective-permute-done.2.behind_ref
  58.1 0.0 copy-start.2
  58.1 0.9 %broadcast_in_dim.10 = bf16[64,2,1152]{2,1,0:T(2,128)(2,1)} broadcast(bf16[2,1152]{1,0:T(2,128)(2,1)S(1)} %reduce_sum.12), dimensions={1,2} | broadcast | bytes 299520 | tf_op jit(solution)/shard_map/broadcast_in_dim | solution.py:539
  59.0 8.8 %all-to-all-start.1 = ((bf16[64,2,1152]{2,1,0:T(2,128)(2,1)}), bf16[64,2,1152]{2,1,0:T(2,128)(2,1)S(1)}, u32[]{:S(2)}, u32[]{:S(2)}) async-start(bf16[64,2,1152]{2,1,0:T(2,128)(2,1)} %broadcast_in_dim.10), calls=%async_computation.1 | async-start | bytes 589824 | tf_op jit(solution)/shard_map/all_to_all | solution.py:541
  67.7 0.0 copy-done.2
  67.8 8.9 %mr_backward.1 = bf16[256,2,1024]{2,1,0:T(2,128)(2,1)} custom-call(bf16[256,1024]{1,0:T(8,128)(2,1)} %get-tuple-element.46.key_grad, bf16[256,1024]{1,0:T(8,128)(2,1)} %get-tuple-element.33.pb.own_ref, f32[128,1024]{1,0:T(8,128)} %mf_ref.3, f32[1,1024]{1,0:T(1,128)} %bitcast.20, bf16[128,1024]{1,0:T(8,128)(2,1)} %copy-done.2, ...), custom_call_target="tpu_custom_call" | custom-call | flops 524288000 | bytes 4194304 | tf_op jit(solution)/shard_map/mr_backward/pallas_call | solution.py:474
  76.6 3.2 %all-to-all-done.1 = bf16[64,2,1152]{2,1,0:T(2,128)(2,1)S(1)} async-done(((bf16[64,2,1152]{2,1,0:T(2,128)(2,1)}), bf16[64,2,1152]{2,1,0:T(2,128)(2,1)S(1)}, u32[]{:S(2)}, u32[]{:S(2)}) %all-to-all-start.1) | async-done | bytes 294944 | tf_op jit(solution)/shard_map/all_to_all | solution.py:541
  79.9 0.6 copy.19
  80.5 0.2 slice.18
  80.7 1.2 %reshape.14 = f32[128,1024]{1,0:T(8,128)} reshape(f32[64,2,1024]{2,1,0:T(2,128)S(1)} %slice.18) | data formatting | bytes 1048576 | tf_op jit(solution)/shard_map/reshape | solution.py:542
  (3 shorter events, 0.0 us)
Async XLA Ops:
  2.5 5.6 %collective-permute-start = (bf16[32,1024]{1,0:T(8,128)(2,1)}, bf16[32,1024]{1,0:T(8,128)(2,1)S(1)}, u32[]{:S(2)}, u32[]{:S(2)}) collective-permute-start(bf16[32,1024]{1,0:T(8,128)(2,1)} %last_rows.1.after_ref.last_ref), channel_id=1, source_target_pairs={{0,4},{4,8},{8,12},{12,16},{16,20},{20,24},{24,28},{28,32},{32,36}... | collective-permute-start | bytes 196616 | tf_op jit(solution)/shard_map/ppermute | solution.py:561
  8.1 1.3 %copy-start.1 = (bf16[32,1024]{1,0:T(8,128)(2,1)}, bf16[32,1024]{1,0:T(8,128)(2,1)S(1)}, u32[]{:S(2)}) copy-start(bf16[32,1024]{1,0:T(8,128)(2,1)S(1)} %collective-permute-done.before_ref) | copy-start | bytes 196612
  8.1 12.3 %collective-permute-start.1 = (bf16[176,1024]{1,0:T(8,128)(2,1)}, bf16[176,1024]{1,0:T(8,128)(2,1)S(1)}, u32[]{:S(2)}, u32[]{:S(2)}) collective-permute-start(bf16[176,1024]{1,0:T(8,128)(2,1)} %first_rows.1), channel_id=1, source_target_pairs={{4,0},{8,4},{12,8},{16,12},{20,16},{24,20},{28,24},{32,28},{36,32}... | collective-permute-start | bytes 1081352 | tf_op jit(solution)/shard_map/ppermute | solution.py:563
  20.5 0.7 copy-start
  21.2 23.2 %copy-start.3 = (bf16[128,1024]{1,0:T(8,128)(2,1)S(1)}, bf16[128,1024]{1,0:T(8,128)(2,1)}, u32[]{:S(2)}) copy-start(bf16[128,1024]{1,0:T(8,128)(2,1)} %get-tuple-element.48) | copy-start | bytes 786436
  30.5 27.3 %all-to-all-start = ((bf16[64,2,1152]{2,1,0:T(2,128)(2,1)}), bf16[64,2,1152]{2,1,0:T(2,128)(2,1)S(1)}, u32[]{:S(2)}, u32[]{:S(2)}) async-start(bf16[64,2,1152]{2,1,0:T(2,128)(2,1)} %get-tuple-element.44), calls=%async_computation | async-start | bytes 589824 | tf_op jit(solution)/shard_map/all_to_all | solution.py:616
  44.4 13.7 %collective-permute-start.2 = (bf16[128,1024]{1,0:T(8,128)(2,1)S(1)}, bf16[128,1024]{1,0:T(8,128)(2,1)S(1)}, u32[]{:S(2)}, u32[]{:S(2)}) collective-permute-start(bf16[128,1024]{1,0:T(8,128)(2,1)S(1)} %copy-done.3), channel_id=1, source_target_pairs={{0,4},{4,8},{8,12},{12,16},{16,20},{20,24},{24,28},{28,32},{32,36}... | collective-permute-start | bytes 786440 | tf_op jit(solution)/shard_map/ppermute | solution.py:614
  58.1 9.6 %copy-start.2 = (bf16[128,1024]{1,0:T(8,128)(2,1)}, bf16[128,1024]{1,0:T(8,128)(2,1)S(1)}, u32[]{:S(2)}) copy-start(bf16[128,1024]{1,0:T(8,128)(2,1)S(1)} %collective-permute-done.2.behind_ref) | copy-start | bytes 786436
  59.0 20.9 %all-to-all-start.1 = ((bf16[64,2,1152]{2,1,0:T(2,128)(2,1)}), bf16[64,2,1152]{2,1,0:T(2,128)(2,1)S(1)}, u32[]{:S(2)}, u32[]{:S(2)}) async-start(bf16[64,2,1152]{2,1,0:T(2,128)(2,1)} %broadcast_in_dim.10), calls=%async_computation.1 | async-start | bytes 589824 | tf_op jit(solution)/shard_map/all_to_all | solution.py:541

commit v4 on v3

--- a/solution.py
+++ b/solution.py
@@ -537,7 +537,6 @@
     channels = width - LANES
     total = jnp.sum(shares.astype(F32), axis=0).astype(BF16)
     copies = jnp.broadcast_to(total[None], shares.shape)
-    copies, behind = lax.optimization_barrier((copies, behind))
     totals = lax.all_to_all(copies, "ctx", 0, 0, tiled=True).reshape(64, 2, width).astype(F32)
     medium_total = totals[:, :, :channels].reshape(count * depth, channels)
     short_total = totals[: channels // 16, 0, channels:].reshape(-1, 8, LANES)
@@ -610,8 +609,8 @@
         4000,
         [jax.ShapeDtypeStruct((64, 2, channels + LANES), BF16)],
     )
-    terms, edge = lax.optimization_barrier((terms, edge))
     behind = lax.ppermute(edge, "ctx", onward)
+    terms, behind = lax.optimization_barrier((terms, behind))
     terms = terms.reshape(count, 128 // count, channels + LANES)
     shares = lax.all_to_all(terms, "ctx", 0, 0, tiled=True)
     se_out, key_grad = blocks_call(

time: 82.4 us -> 79.2 us (0.961)
  waiting for transfers between devices: 10.5 us -> 8.64 us
  starting transfers between devices: 30.6 us -> 29.3 us
    all_to_all x1, starting transfers between devices: 8.76 us -> 5.21 us  [ctx_totals(): lax.all_to_all(copies, 'ctx', 0, 0, tiled=True).reshape(64, 2, width)]
    ppermute x1, waiting for transfers between devices: 3.31 us -> 0.01 us  [local(): ahead = lax.ppermute(first, 'ctx', backward)]
    all_to_all x1, waiting for transfers between devices: 4 us -> 6.03 us  [local(): shares = lax.all_to_all(terms, 'ctx', 0, 0, tiled=True)]
    ppermute x1, starting transfers between devices: 3.49 us -> 4.65 us  [local(): behind = lax.ppermute(edge, 'ctx', onward)]
    all_to_all x1, starting transfers between devices: 13.9 us -> 14.9 us  [local(): shares = lax.all_to_all(terms, 'ctx', 0, 0, tiled=True)]
  transfers between devices with their start and end apart: 5 -> 5, of which waited for: 3 -> 2; matrix products, arithmetic and copies ran while one was open for 0% -> 0% of each run, Pallas kernels for 31% -> 44%
where the time goes in v4:
time: 79.2 us; the launch traced here: 78.6 us
  Pallas kernels  36.1 us (46%)
  starting transfers between devices  29.3 us (37%)
  waiting for transfers between devices  8.64 us (11%)
  local copies, waits for them, and re-layouts  3.6 us (5%)
    pallas_call x4, Pallas kernels, blocks_call(): pl.pallas_call(body, grid=(channels // BLOCK,), in_specs=[rows_of(*a.shap...  31.8 us
    all_to_all x1, starting transfers between devices, local(): shares = lax.all_to_all(terms, 'ctx', 0, 0, tiled=True)  14.9 us
    all_to_all x1, waiting for transfers between devices, local(): shares = lax.all_to_all(terms, 'ctx', 0, 0, tiled=True)  6.03 us
    all_to_all x1, starting transfers between devices, ctx_totals(): lax.all_to_all(copies, 'ctx', 0, 0, tiled=True).reshape(64, 2, width)  5.21 us
    ppermute x1, starting transfers between devices, local(): behind = lax.ppermute(edge, 'ctx', onward)  4.65 us
    pallas_call x2, Pallas kernels, edge_call(): pl.pallas_call(body, grid=(channels // wide,), in_specs=[pairs(count, at)...  4.3 us
    ppermute x1, starting transfers between devices, local(): before = lax.ppermute(last, 'ctx', onward)  3.18 us
    all_to_all x1, waiting for transfers between devices, ctx_totals(): lax.all_to_all(copies, 'ctx', 0, 0, tiled=True).reshape(64, 2, width)  2.6 us
  transfers between devices with their start and end apart: 5, of which 2 were waited for; matrix products, arithmetic and copies ran while one was open for 0% of the time, Pallas kernels for 44%

profile of v4, /device:TPU:16, one launch (start us, length us, event | category | flops | bytes accessed | tf_op | source)
XLA Modules:
  0.0 78.6 jit_solution(5547031857949390567)
XLA Ops:
  0.6 1.8 %last_rows.1.after_ref.last_ref = bf16[32,1024]{1,0:T(8,128)(2,1)} custom-call(bf16[3,256,1024]{2,1,0:T(8,128)(2,1)} %bitcast.12, bf16[256,2,1024]{2,1,0:T(2,128)(2,1)} %mr_ref.1, f32[3,3,1024]{2,1,0:T(4,128)} %sw_ref.7, f32[7,1024]{1,0:T(8,128)} %sf_ref.7), custom_call_target="tpu_custom_call" | custom-call | tf_op jit(solution)/shard_map/last_rows/pallas_call | solution.py:501
  2.5 3.2 %collective-permute-start = (bf16[32,1024]{1,0:T(8,128)(2,1)}, bf16[32,1024]{1,0:T(8,128)(2,1)S(1)}, u32[]{:S(2)}, u32[]{:S(2)}) collective-permute-start(bf16[32,1024]{1,0:T(8,128)(2,1)} %last_rows.1.after_ref.last_ref), channel_id=1, source_target_pairs={{0,4},{4,8},{8,12},{12,16},{16,20},{20,24},{24,28},{28,32},{32,36}... | collective-permute-start | bytes 196616 | tf_op jit(solution)/shard_map/ppermute | solution.py:560
  5.7 2.5 %first_rows.1 = bf16[176,1024]{1,0:T(8,128)(2,1)} custom-call(bf16[3,256,1024]{2,1,0:T(8,128)(2,1)} %bitcast.13, bf16[256,2,1024]{2,1,0:T(2,128)(2,1)} %mr_ref.1, bf16[256,1024]{1,0:T(8,128)(2,1)} %g_ref.5, f32[3,3,1024]{2,1,0:T(4,128)} %mw_ref.9, bf16[32,1024]{1,0:T(8,128)(2,1)} %last_rows.1.after_ref.last_ref), custom_call_target="tpu_custom_call" | custom-call | tf_op jit(solution)/shard_map/first_rows/pallas_call | solution.py:501
  8.1 0.0 collective-permute-done.before_ref
  8.1 0.0 copy-start.1
  8.1 1.3 %collective-permute-start.1 = (bf16[176,1024]{1,0:T(8,128)(2,1)}, bf16[176,1024]{1,0:T(8,128)(2,1)S(1)}, u32[]{:S(2)}, u32[]{:S(2)}) collective-permute-start(bf16[176,1024]{1,0:T(8,128)(2,1)} %first_rows.1), channel_id=1, source_target_pairs={{4,0},{8,4},{12,8},{16,12},{20,16},{24,20},{28,24},{32,28},{36,32}... | collective-permute-start | bytes 1081352 | tf_op jit(solution)/shard_map/ppermute | solution.py:562
  9.4 0.0 copy-done.1
  9.4 7.7 %forward.1 = (f32[256,1024]{1,0:T(8,128)}, f32[256,1024]{1,0:T(8,128)}, f32[256,1024]{1,0:T(8,128)}, f32[256,1024]{1,0:T(8,128)}, bf16[256,1024]{1,0:T(8,128)(2,...) custom-call(bf16[3,256,1024]{2,1,0:T(8,128)(2,1)} %bitcast.14, ...), custom_call_target="tpu_custom_call" | custom-call | flops 1048576000 | bytes 4194304 | tf_op jit(solution)/shard_map/forward/pallas_call | solution.py:474
  17.1 4.6 %collective-permute-start.2 = (bf16[128,1024]{1,0:T(8,128)(2,1)}, bf16[128,1024]{1,0:T(8,128)(2,1)S(1)}, u32[]{:S(2)}, u32[]{:S(2)}) collective-permute-start(bf16[128,1024]{1,0:T(8,128)(2,1)} %get-tuple-element.41), channel_id=1, source_target_pairs={{0,4},{4,8},{8,12},{12,16},{16,20},{20,24},{24,28},{28,32},{32,36}... | collective-permute-start | bytes 786440 | tf_op jit(solution)/shard_map/ppermute | solution.py:612
  21.8 0.0 collective-permute-done.1.ahead_ref
  21.8 0.0 copy-start
  21.8 0.7 copy-done
  22.6 9.3 %middle.1 = (f32[272,1024]{1,0:T(8,128)}, f32[272,1024]{1,0:T(8,128)}, f32[5,16,1024]{2,1,0:T(8,128)}, f32[16,1024]{1,0:T(8,128)}, bf16[16,1024]{1,0:T(8,128)(2,1)}, /*index=5*/bf16[64,2,1152]{2,1,0:T(2,128)(2,1)}) custom-call(f32[256,1024]{1,0:T(8,128)} %get-tuple-element.27.q1_ref, f32[256,1024]{1,0:T(8,128)} %get-tuple-element.29.k2_ref, ...), custom_call_target="tpu_custom_call" | custom-call | flops 1048576000 | bytes 4194304 | tf_op jit(solution)/shard_map/middle/pallas_call | solution.py:474
  31.8 0.0 collective-permute-done.2.behind_ref
  31.8 0.0 copy-start.2
  31.8 14.9 %all-to-all-start = ((bf16[64,2,1152]{2,1,0:T(2,128)(2,1)}), bf16[64,2,1152]{2,1,0:T(2,128)(2,1)S(1)}, u32[]{:S(2)}, u32[]{:S(2)}) async-start(bf16[64,2,1152]{2,1,0:T(2,128)(2,1)} %get-tuple-element.42), calls=%async_computation | async-start | bytes 589824 | tf_op jit(solution)/shard_map/all_to_all | solution.py:615
  46.8 5.9 %se_backward.1 = (bf16[3,256,1024]{2,1,0:T(8,128)(2,1)}, bf16[256,1024]{1,0:T(8,128)(2,1)}) custom-call(f32[256,1024]{1,0:T(8,128)} %get-tuple-element.27.q1_ref, f32[256,1024]{1,0:T(8,128)} %get-tuple-element.28.z1_ref, f32[5,16,1024]{2,1,0:T(8,128)} %get-tuple-element.34.feats_ahead, f32[256,1024]{1,0:T(8,128)} %get-tuple-element.35.v2, ...), custom_call_target="tpu_custom_call" | custom-call | flops 524288000 | bytes 4194304 | tf_op jit(solution)/shard_map/se_backward/pallas_call | solution.py:474
  52.7 0.0 copy-done.2
  52.7 6.0 %all-to-all-done = bf16[64,2,1152]{2,1,0:T(2,128)(2,1)S(1)} async-done(((bf16[64,2,1152]{2,1,0:T(2,128)(2,1)}), bf16[64,2,1152]{2,1,0:T(2,128)(2,1)S(1)}, u32[]{:S(2)}, u32[]{:S(2)}) %all-to-all-start) | async-done | bytes 294944 | tf_op jit(solution)/shard_map/all_to_all | solution.py:615
  58.8 0.3 reduce_sum.12
  59.0 0.9 %broadcast_in_dim.10 = bf16[64,2,1152]{2,1,0:T(2,128)(2,1)} broadcast(bf16[2,1152]{1,0:T(2,128)(2,1)S(1)} %reduce_sum.12), dimensions={1,2} | broadcast | bytes 299520 | tf_op jit(solution)/shard_map/broadcast_in_dim | solution.py:539
  59.9 5.2 %all-to-all-start.1 = ((bf16[64,2,1152]{2,1,0:T(2,128)(2,1)}), bf16[64,2,1152]{2,1,0:T(2,128)(2,1)S(1)}, u32[]{:S(2)}, u32[]{:S(2)}) async-start(bf16[64,2,1152]{2,1,0:T(2,128)(2,1)} %broadcast_in_dim.10), calls=%async_computation.1 | async-start | bytes 589824 | tf_op jit(solution)/shard_map/all_to_all | solution.py:540
  65.1 8.9 %mr_backward.1 = bf16[256,2,1024]{2,1,0:T(2,128)(2,1)} custom-call(bf16[256,1024]{1,0:T(8,128)(2,1)} %get-tuple-element.44.key_grad, bf16[256,1024]{1,0:T(8,128)(2,1)} %get-tuple-element.31.pb.own_ref, f32[128,1024]{1,0:T(8,128)} %mf_ref.3, f32[1,1024]{1,0:T(1,128)} %bitcast.20, bf16[128,1024]{1,0:T(8,128)(2,1)} %copy-done.2, ...), custom_call_target="tpu_custom_call" | custom-call | flops 524288000 | bytes 4194304 | tf_op jit(solution)/shard_map/mr_backward/pallas_call | solution.py:474
  74.0 2.6 %all-to-all-done.1 = bf16[64,2,1152]{2,1,0:T(2,128)(2,1)S(1)} async-done(((bf16[64,2,1152]{2,1,0:T(2,128)(2,1)}), bf16[64,2,1152]{2,1,0:T(2,128)(2,1)S(1)}, u32[]{:S(2)}, u32[]{:S(2)}) %all-to-all-start.1) | async-done | bytes 294944 | tf_op jit(solution)/shard_map/all_to_all | solution.py:540
  76.7 0.6 copy.19
  77.3 0.2 slice.18
  77.5 1.2 %reshape.14 = f32[128,1024]{1,0:T(8,128)} reshape(f32[64,2,1024]{2,1,0:T(2,128)S(1)} %slice.18) | data formatting | bytes 1048576 | tf_op jit(solution)/shard_map/reshape | solution.py:541
  (3 shorter events, 0.0 us)
Async XLA Ops:
  2.5 5.6 %collective-permute-start = (bf16[32,1024]{1,0:T(8,128)(2,1)}, bf16[32,1024]{1,0:T(8,128)(2,1)S(1)}, u32[]{:S(2)}, u32[]{:S(2)}) collective-permute-start(bf16[32,1024]{1,0:T(8,128)(2,1)} %last_rows.1.after_ref.last_ref), channel_id=1, source_target_pairs={{0,4},{4,8},{8,12},{12,16},{16,20},{20,24},{24,28},{28,32},{32,36}... | collective-permute-start | bytes 196616 | tf_op jit(solution)/shard_map/ppermute | solution.py:560
  8.1 1.3 %copy-start.1 = (bf16[32,1024]{1,0:T(8,128)(2,1)}, bf16[32,1024]{1,0:T(8,128)(2,1)S(1)}, u32[]{:S(2)}) copy-start(bf16[32,1024]{1,0:T(8,128)(2,1)S(1)} %collective-permute-done.before_ref) | copy-start | bytes 196612
  8.1 13.7 %collective-permute-start.1 = (bf16[176,1024]{1,0:T(8,128)(2,1)}, bf16[176,1024]{1,0:T(8,128)(2,1)S(1)}, u32[]{:S(2)}, u32[]{:S(2)}) collective-permute-start(bf16[176,1024]{1,0:T(8,128)(2,1)} %first_rows.1), channel_id=1, source_target_pairs={{4,0},{8,4},{12,8},{16,12},{20,16},{24,20},{28,24},{32,28},{36,32}... | collective-permute-start | bytes 1081352 | tf_op jit(solution)/shard_map/ppermute | solution.py:562
  17.1 14.7 %collective-permute-start.2 = (bf16[128,1024]{1,0:T(8,128)(2,1)}, bf16[128,1024]{1,0:T(8,128)(2,1)S(1)}, u32[]{:S(2)}, u32[]{:S(2)}) collective-permute-start(bf16[128,1024]{1,0:T(8,128)(2,1)} %get-tuple-element.41), channel_id=1, source_target_pairs={{0,4},{4,8},{8,12},{12,16},{16,20},{20,24},{24,28},{28,32},{32,36}... | collective-permute-start | bytes 786440 | tf_op jit(solution)/shard_map/ppermute | solution.py:612
  21.8 0.7 copy-start
  31.8 20.9 %copy-start.2 = (bf16[128,1024]{1,0:T(8,128)(2,1)}, bf16[128,1024]{1,0:T(8,128)(2,1)S(1)}, u32[]{:S(2)}) copy-start(bf16[128,1024]{1,0:T(8,128)(2,1)S(1)} %collective-permute-done.2.behind_ref) | copy-start | bytes 786436
  31.8 26.9 %all-to-all-start = ((bf16[64,2,1152]{2,1,0:T(2,128)(2,1)}), bf16[64,2,1152]{2,1,0:T(2,128)(2,1)S(1)}, u32[]{:S(2)}, u32[]{:S(2)}) async-start(bf16[64,2,1152]{2,1,0:T(2,128)(2,1)} %get-tuple-element.42), calls=%async_computation | async-start | bytes 589824 | tf_op jit(solution)/shard_map/all_to_all | solution.py:615
  59.9 16.7 %all-to-all-start.1 = ((bf16[64,2,1152]{2,1,0:T(2,128)(2,1)}), bf16[64,2,1152]{2,1,0:T(2,128)(2,1)S(1)}, u32[]{:S(2)}, u32[]{:S(2)}) async-start(bf16[64,2,1152]{2,1,0:T(2,128)(2,1)} %broadcast_in_dim.10), calls=%async_computation.1 | async-start | bytes 589824 | tf_op jit(solution)/shard_map/all_to_all | solution.py:540

commit v5 on v4

--- a/solution.py
+++ b/solution.py
@@ -13,7 +13,7 @@
 F32 = jnp.float32
 BF16 = jnp.bfloat16
 LANES = 128
-BLOCK = 256
+BLOCK = 512
 PAD = 16
 LIMIT = 56 * 2**20
 REACH = 16

time: 79.2 us -> 78.6 us (level)
  Pallas kernels: 36.1 us -> 33.9 us
  waiting for transfers between devices: 8.64 us -> 10.6 us
    pallas_call x4, Pallas kernels: 31.8 us -> 29.5 us  [blocks_call(): pl.pallas_call(body, grid=(channels // BLOCK,), in_specs=[rows_of(*a.shap...]
    all_to_all x1, waiting for transfers between devices: 2.6 us -> 4.28 us  [ctx_totals(): lax.all_to_all(copies, 'ctx', 0, 0, tiled=True).reshape(64, 2, width)]
  transfers between devices with their start and end apart: 5 -> 5, of which waited for: 2 -> 2; matrix products, arithmetic and copies ran while one was open for 0% -> 0% of each run, Pallas kernels for 44% -> 41%
where the time goes in v5:
time: 78.6 us; the launch traced here: 78.3 us
  Pallas kernels  33.9 us (43%)
  starting transfers between devices  29.2 us (37%)
  waiting for transfers between devices  10.6 us (13%)
  local copies, waits for them, and re-layouts  3.6 us (5%)
    pallas_call x4, Pallas kernels, blocks_call(): pl.pallas_call(body, grid=(channels // BLOCK,), in_specs=[rows_of(*a.shap...  29.5 us
    all_to_all x1, starting transfers between devices, local(): shares = lax.all_to_all(terms, 'ctx', 0, 0, tiled=True)  14.9 us
    all_to_all x1, waiting for transfers between devices, local(): shares = lax.all_to_all(terms, 'ctx', 0, 0, tiled=True)  6.29 us
    all_to_all x1, starting transfers between devices, ctx_totals(): lax.all_to_all(copies, 'ctx', 0, 0, tiled=True).reshape(64, 2, width)  5.15 us
    ppermute x1, starting transfers between devices, local(): behind = lax.ppermute(edge, 'ctx', onward)  4.64 us
    pallas_call x2, Pallas kernels, edge_call(): pl.pallas_call(body, grid=(channels // wide,), in_specs=[pairs(count, at)...  4.3 us
    all_to_all x1, waiting for transfers between devices, ctx_totals(): lax.all_to_all(copies, 'ctx', 0, 0, tiled=True).reshape(64, 2, width)  4.28 us
    ppermute x1, starting transfers between devices, local(): before = lax.ppermute(last, 'ctx', onward)  3.18 us
  transfers between devices with their start and end apart: 5, of which 2 were waited for; matrix products, arithmetic and copies ran while one was open for 0% of the time, Pallas kernels for 41%

profile of v5, /device:TPU:16, one launch (start us, length us, event | category | flops | bytes accessed | tf_op | source)
XLA Modules:
  0.0 78.3 jit_solution(1646116322522141381)
XLA Ops:
  0.6 1.8 %last_rows.1.after_ref.last_ref = bf16[32,1024]{1,0:T(8,128)(2,1)} custom-call(bf16[3,256,1024]{2,1,0:T(8,128)(2,1)} %bitcast.12, bf16[256,2,1024]{2,1,0:T(2,128)(2,1)} %mr_ref.1, f32[3,3,1024]{2,1,0:T(4,128)} %sw_ref.7, f32[7,1024]{1,0:T(8,128)} %sf_ref.7), custom_call_target="tpu_custom_call" | custom-call | tf_op jit(solution)/shard_map/last_rows/pallas_call | solution.py:501
  2.5 3.2 %collective-permute-start = (bf16[32,1024]{1,0:T(8,128)(2,1)}, bf16[32,1024]{1,0:T(8,128)(2,1)S(1)}, u32[]{:S(2)}, u32[]{:S(2)}) collective-permute-start(bf16[32,1024]{1,0:T(8,128)(2,1)} %last_rows.1.after_ref.last_ref), channel_id=1, source_target_pairs={{0,4},{4,8},{8,12},{12,16},{16,20},{20,24},{24,28},{28,32},{32,36}... | collective-permute-start | bytes 196616 | tf_op jit(solution)/shard_map/ppermute | solution.py:560
  5.7 2.5 %first_rows.1 = bf16[176,1024]{1,0:T(8,128)(2,1)} custom-call(bf16[3,256,1024]{2,1,0:T(8,128)(2,1)} %bitcast.13, bf16[256,2,1024]{2,1,0:T(2,128)(2,1)} %mr_ref.1, bf16[256,1024]{1,0:T(8,128)(2,1)} %g_ref.5, f32[3,3,1024]{2,1,0:T(4,128)} %mw_ref.9, bf16[32,1024]{1,0:T(8,128)(2,1)} %last_rows.1.after_ref.last_ref), custom_call_target="tpu_custom_call" | custom-call | tf_op jit(solution)/shard_map/first_rows/pallas_call | solution.py:501
  8.1 0.0 collective-permute-done.before_ref
  8.1 0.0 copy-start.1
  8.1 1.3 %collective-permute-start.1 = (bf16[176,1024]{1,0:T(8,128)(2,1)}, bf16[176,1024]{1,0:T(8,128)(2,1)S(1)}, u32[]{:S(2)}, u32[]{:S(2)}) collective-permute-start(bf16[176,1024]{1,0:T(8,128)(2,1)} %first_rows.1), channel_id=1, source_target_pairs={{4,0},{8,4},{12,8},{16,12},{20,16},{24,20},{28,24},{32,28},{36,32}... | collective-permute-start | bytes 1081352 | tf_op jit(solution)/shard_map/ppermute | solution.py:562
  9.4 0.0 copy-done.1
  9.4 8.1 %forward.1 = (f32[256,1024]{1,0:T(8,128)}, f32[256,1024]{1,0:T(8,128)}, f32[256,1024]{1,0:T(8,128)}, f32[256,1024]{1,0:T(8,128)}, bf16[256,1024]{1,0:T(8,128)(2,...) custom-call(bf16[3,256,1024]{2,1,0:T(8,128)(2,1)} %bitcast.14, ...), custom_call_target="tpu_custom_call" | custom-call | flops 1048576000 | bytes 4194304 | tf_op jit(solution)/shard_map/forward/pallas_call | solution.py:474
  17.6 4.6 %collective-permute-start.2 = (bf16[128,1024]{1,0:T(8,128)(2,1)}, bf16[128,1024]{1,0:T(8,128)(2,1)S(1)}, u32[]{:S(2)}, u32[]{:S(2)}) collective-permute-start(bf16[128,1024]{1,0:T(8,128)(2,1)} %get-tuple-element.41), channel_id=1, source_target_pairs={{0,4},{4,8},{8,12},{12,16},{16,20},{20,24},{24,28},{28,32},{32,36}... | collective-permute-start | bytes 786440 | tf_op jit(solution)/shard_map/ppermute | solution.py:612
  22.2 0.0 collective-permute-done.1.ahead_ref
  22.2 0.0 copy-start
  22.2 0.7 copy-done
  23.0 8.7 %middle.1 = (f32[272,1024]{1,0:T(8,128)}, f32[272,1024]{1,0:T(8,128)}, f32[5,16,1024]{2,1,0:T(8,128)}, f32[16,1024]{1,0:T(8,128)}, bf16[16,1024]{1,0:T(8,128)(2,1)}, /*index=5*/bf16[64,2,1152]{2,1,0:T(2,128)(2,1)}) custom-call(f32[256,1024]{1,0:T(8,128)} %get-tuple-element.27.q1_ref, f32[256,1024]{1,0:T(8,128)} %get-tuple-element.29.k2_ref, ...), custom_call_target="tpu_custom_call" | custom-call | flops 1048576000 | bytes 4194304 | tf_op jit(solution)/shard_map/middle/pallas_call | solution.py:474
  31.7 0.0 collective-permute-done.2.behind_ref
  31.7 0.0 copy-start.2
  31.7 14.9 %all-to-all-start = ((bf16[64,2,1152]{2,1,0:T(2,128)(2,1)}), bf16[64,2,1152]{2,1,0:T(2,128)(2,1)S(1)}, u32[]{:S(2)}, u32[]{:S(2)}) async-start(bf16[64,2,1152]{2,1,0:T(2,128)(2,1)} %get-tuple-element.42), calls=%async_computation | async-start | bytes 589824 | tf_op jit(solution)/shard_map/all_to_all | solution.py:615
  46.7 5.7 %se_backward.1 = (bf16[3,256,1024]{2,1,0:T(8,128)(2,1)}, bf16[256,1024]{1,0:T(8,128)(2,1)}) custom-call(f32[256,1024]{1,0:T(8,128)} %get-tuple-element.27.q1_ref, f32[256,1024]{1,0:T(8,128)} %get-tuple-element.28.z1_ref, f32[5,16,1024]{2,1,0:T(8,128)} %get-tuple-element.34.feats_ahead, f32[256,1024]{1,0:T(8,128)} %get-tuple-element.35.v2, ...), custom_call_target="tpu_custom_call" | custom-call | flops 524288000 | bytes 4194304 | tf_op jit(solution)/shard_map/se_backward/pallas_call | solution.py:474
  52.3 0.0 copy-done.2
  52.3 6.3 %all-to-all-done = bf16[64,2,1152]{2,1,0:T(2,128)(2,1)S(1)} async-done(((bf16[64,2,1152]{2,1,0:T(2,128)(2,1)}), bf16[64,2,1152]{2,1,0:T(2,128)(2,1)S(1)}, u32[]{:S(2)}, u32[]{:S(2)}) %all-to-all-start) | async-done | bytes 294944 | tf_op jit(solution)/shard_map/all_to_all | solution.py:615
  58.6 0.3 reduce_sum.12
  58.9 0.9 %broadcast_in_dim.10 = bf16[64,2,1152]{2,1,0:T(2,128)(2,1)} broadcast(bf16[2,1152]{1,0:T(2,128)(2,1)S(1)} %reduce_sum.12), dimensions={1,2} | broadcast | bytes 299520 | tf_op jit(solution)/shard_map/broadcast_in_dim | solution.py:539
  59.8 5.1 %all-to-all-start.1 = ((bf16[64,2,1152]{2,1,0:T(2,128)(2,1)}), bf16[64,2,1152]{2,1,0:T(2,128)(2,1)S(1)}, u32[]{:S(2)}, u32[]{:S(2)}) async-start(bf16[64,2,1152]{2,1,0:T(2,128)(2,1)} %broadcast_in_dim.10), calls=%async_computation.1 | async-start | bytes 589824 | tf_op jit(solution)/shard_map/all_to_all | solution.py:540
  64.9 7.1 %mr_backward.1 = bf16[256,2,1024]{2,1,0:T(2,128)(2,1)} custom-call(bf16[256,1024]{1,0:T(8,128)(2,1)} %get-tuple-element.44.key_grad, bf16[256,1024]{1,0:T(8,128)(2,1)} %get-tuple-element.31.pb.own_ref, f32[128,1024]{1,0:T(8,128)} %mf_ref.3, f32[1,1024]{1,0:T(1,128)} %bitcast.20, bf16[128,1024]{1,0:T(8,128)(2,1)} %copy-done.2, ...), custom_call_target="tpu_custom_call" | custom-call | flops 524288000 | bytes 4194304 | tf_op jit(solution)/shard_map/mr_backward/pallas_call | solution.py:474
  72.0 4.3 %all-to-all-done.1 = bf16[64,2,1152]{2,1,0:T(2,128)(2,1)S(1)} async-done(((bf16[64,2,1152]{2,1,0:T(2,128)(2,1)}), bf16[64,2,1152]{2,1,0:T(2,128)(2,1)S(1)}, u32[]{:S(2)}, u32[]{:S(2)}) %all-to-all-start.1) | async-done | bytes 294944 | tf_op jit(solution)/shard_map/all_to_all | solution.py:540
  76.3 0.6 copy.19
  76.9 0.2 slice.18
  77.1 1.2 %reshape.14 = f32[128,1024]{1,0:T(8,128)} reshape(f32[64,2,1024]{2,1,0:T(2,128)S(1)} %slice.18) | data formatting | bytes 1048576 | tf_op jit(solution)/shard_map/reshape | solution.py:541
  (3 shorter events, 0.0 us)
Async XLA Ops:
  2.5 5.6 %collective-permute-start = (bf16[32,1024]{1,0:T(8,128)(2,1)}, bf16[32,1024]{1,0:T(8,128)(2,1)S(1)}, u32[]{:S(2)}, u32[]{:S(2)}) collective-permute-start(bf16[32,1024]{1,0:T(8,128)(2,1)} %last_rows.1.after_ref.last_ref), channel_id=1, source_target_pairs={{0,4},{4,8},{8,12},{12,16},{16,20},{20,24},{24,28},{28,32},{32,36}... | collective-permute-start | bytes 196616 | tf_op jit(solution)/shard_map/ppermute | solution.py:560
  8.1 1.3 %copy-start.1 = (bf16[32,1024]{1,0:T(8,128)(2,1)}, bf16[32,1024]{1,0:T(8,128)(2,1)S(1)}, u32[]{:S(2)}) copy-start(bf16[32,1024]{1,0:T(8,128)(2,1)S(1)} %collective-permute-done.before_ref) | copy-start | bytes 196612
  8.1 14.1 %collective-permute-start.1 = (bf16[176,1024]{1,0:T(8,128)(2,1)}, bf16[176,1024]{1,0:T(8,128)(2,1)S(1)}, u32[]{:S(2)}, u32[]{:S(2)}) collective-permute-start(bf16[176,1024]{1,0:T(8,128)(2,1)} %first_rows.1), channel_id=1, source_target_pairs={{4,0},{8,4},{12,8},{16,12},{20,16},{24,20},{28,24},{32,28},{36,32}... | collective-permute-start | bytes 1081352 | tf_op jit(solution)/shard_map/ppermute | solution.py:562
  17.6 14.1 %collective-permute-start.2 = (bf16[128,1024]{1,0:T(8,128)(2,1)}, bf16[128,1024]{1,0:T(8,128)(2,1)S(1)}, u32[]{:S(2)}, u32[]{:S(2)}) collective-permute-start(bf16[128,1024]{1,0:T(8,128)(2,1)} %get-tuple-element.41), channel_id=1, source_target_pairs={{0,4},{4,8},{8,12},{12,16},{16,20},{20,24},{24,28},{28,32},{32,36}... | collective-permute-start | bytes 786440 | tf_op jit(solution)/shard_map/ppermute | solution.py:612
  22.2 0.7 copy-start
  31.7 20.6 %copy-start.2 = (bf16[128,1024]{1,0:T(8,128)(2,1)}, bf16[128,1024]{1,0:T(8,128)(2,1)S(1)}, u32[]{:S(2)}) copy-start(bf16[128,1024]{1,0:T(8,128)(2,1)S(1)} %collective-permute-done.2.behind_ref) | copy-start | bytes 786436
  31.7 26.9 %all-to-all-start = ((bf16[64,2,1152]{2,1,0:T(2,128)(2,1)}), bf16[64,2,1152]{2,1,0:T(2,128)(2,1)S(1)}, u32[]{:S(2)}, u32[]{:S(2)}) async-start(bf16[64,2,1152]{2,1,0:T(2,128)(2,1)} %get-tuple-element.42), calls=%async_computation | async-start | bytes 589824 | tf_op jit(solution)/shard_map/all_to_all | solution.py:615
  59.8 16.5 %all-to-all-start.1 = ((bf16[64,2,1152]{2,1,0:T(2,128)(2,1)}), bf16[64,2,1152]{2,1,0:T(2,128)(2,1)S(1)}, u32[]{:S(2)}, u32[]{:S(2)}) async-start(bf16[64,2,1152]{2,1,0:T(2,128)(2,1)} %broadcast_in_dim.10), calls=%async_computation.1 | async-start | bytes 589824 | tf_op jit(solution)/shard_map/all_to_all | solution.py:540
